TPU v7x, 256 devices: a whole 4x4x8 slice. The times are simulated.
256 devices in a mesh: group: 16 (over x, y), tensor: 16 (over z, core).
Axes of the slice: x: 4, y: 4, z: 8, core: 2. Of those that a mesh axis runs over, the one named last changes fastest.
Arguments:
- attended: bfloat16 [6144, 6144], P('group', 'tensor'), may hold values from -6 to 6
- out_weight: bfloat16 [6144, 3072], P('tensor'), may hold values from -0.078125 to 0.078125
- feedback_error: float32 [16, 6144, 3072], P('group', 'tensor'), may hold values from -112 to 112
- right_init: float32 [3072, 32], replicated, may hold values from -6 to 6
- cotangent: bfloat16 [6144, 3072], P(('group', 'tensor')), may hold values from -6 to 6
Outputs:
- projected: bfloat16 [6144, 3072], P(('group', 'tensor'))
- input_grad: bfloat16 [6144, 6144], P('group', 'tensor')
- new_error: float32 [16, 6144, 3072], P('group', 'tensor')
- left_factor: float32 [6144, 32], P('tensor')
- right_factor: float32 [3072, 32], replicated
All inputs are finite; a program needn't handle non-finite values.
Results may differ from a plain program's by a relative error of at most 0.008.
Values may be sent and summed in bfloat16 or wider, within the bound.
A program may use at most 64 MiB of HBM per device.

v0:
```python
import jax
import jax.numpy as jnp
from jax import lax
from jax.sharding import PartitionSpec as P


def per_device(attended, out_weight, feedback_error, right_init, cotangent):
    highest = lax.Precision.HIGHEST
    group_count = lax.axis_size("group")
    rank_cols = right_init.shape[1]
    projected = lax.psum_scatter(
        jnp.dot(attended, out_weight, preferred_element_type=jnp.float32),
        "tensor",
        scatter_dimension=0,
        tiled=True,
    ).astype(jnp.bfloat16)
    piece = lax.all_gather(cotangent, "tensor", axis=0, tiled=True)
    collected = piece
    back_piece = lax.dot_general(
        piece, out_weight, (((1,), (1,)), ((), ())), preferred_element_type=jnp.float32
    )
    back_rows = back_piece
    back_rows, collected = (back_rows, collected)
    input_grad = back_rows.astype(jnp.bfloat16)
    grad_sum = lax.dot_general(
        attended, collected, (((0,), (0,)), ((), ())), preferred_element_type=jnp.float32
    )
    moment = grad_sum + feedback_error[0]
    raw_left = lax.psum(jnp.dot(moment, right_init, precision=highest), "group") / group_count
    width_block = rank_cols // 4
    finished = []
    for block_index in range(4):
        column_block = raw_left[:, block_index * width_block : (block_index + 1) * width_block]
        if block_index > 0:
            earlier = jnp.concatenate(finished, axis=1)
            correlation = lax.psum(jnp.dot(earlier.T, column_block, precision=highest), "tensor")
            column_block = column_block - jnp.dot(earlier, correlation, precision=highest)
        block_gram = lax.psum(jnp.dot(column_block.T, column_block, precision=highest), "tensor")
        block_lower = jnp.linalg.cholesky(block_gram)
        finished.append(
            jax.scipy.linalg.solve_triangular(block_lower, column_block.T, lower=True).T
        )
    left_factor = jnp.concatenate(finished, axis=1)
    right_term = jnp.dot(moment.T, left_factor, precision=highest)
    right_factor = lax.psum(right_term, ("group", "tensor")) / group_count
    new_error = (moment - jnp.dot(left_factor, right_factor.T, precision=highest))[None]
    return (projected, input_grad, new_error, left_factor, right_factor)


def solution(mesh):
    in_specs = (
        P("group", "tensor"),
        P("tensor", None),
        P("group", "tensor", None),
        P(),
        P(("group", "tensor"), None),
    )
    out_specs = (
        P(("group", "tensor"), None),
        P("group", "tensor"),
        P("group", "tensor", None),
        P("tensor", None),
        P(),
    )
    return jax.shard_map(
        per_device, mesh=mesh, in_specs=in_specs, out_specs=out_specs, check_vma=False
    )
```

profile of v0, /device:TPU:1, one launch (start us, length us, event | category | flops | bytes accessed | tf_op | source)
XLA Modules:
  0.0 657.8 jit_solution(11114478664006824806)
XLA Ops:
  8.0 46.0 %all-gather.2.cloned.1.call-done = bf16[384,3072]{1,0:T(8,128)(2,1)} async-done(((bf16[24,3072]{1,0:T(8,128)(2,1)}), bf16[384,3072]{1,0:T(8,128)(2,1)}) %all-gather.2.cloned.1.call-update) | async-done | bytes 2359312 | tf_op jit(solution)/shard_map/all_gather | solution.py:17
  54.0 4.7 bitcast_add_fusion
  58.7 2.2 copy-done.1
  60.9 4.3 fusion.31
  65.2 60.5 %psum.63 = f32[384,32]{0,1:T(8,128)S(1)} all-reduce(f32[384,32]{0,1:T(8,128)S(1)} %fusion.31), channel_id=1, replica_groups=mesh['group'=16,'tensor'=16] {'group'}, use_global_device_ids=true, to_apply=%region_1.0 | all-reduce | flops 12288 | bytes 98304 | tf_op jit(solution)/shard_map/psum | solution.py:29
  125.9 37.0 %psum.64 = f32[8,8]{0,1:T(8,128)S(1)} all-reduce(f32[8,8]{0,1:T(8,128)S(1)} %fusion.12), channel_id=1, replica_groups=mesh['group'=16,'tensor'=16] {'tensor'}, use_global_device_ids=true, to_apply=%region_2.0 | all-reduce | flops 64 | bytes 512 | tf_op jit(solution)/shard_map/psum | solution.py:38
  163.0 0.7 cholesky.74
  166.0 23.6 %psum.65 = f32[8,8]{1,0:T(8,128)S(1)} all-reduce(f32[8,8]{1,0:T(8,128)S(1)} %fusion.9), channel_id=1, replica_groups=mesh['group'=16,'tensor'=16] {'tensor'}, use_global_device_ids=true, to_apply=%region_5.0 | all-reduce | flops 64 | bytes 512 | tf_op jit(solution)/shard_map/psum | solution.py:36
  189.9 23.6 %psum.66 = f32[8,8]{0,1:T(8,128)S(1)} all-reduce(f32[8,8]{0,1:T(8,128)S(1)} %fusion.32), channel_id=1, replica_groups=mesh['group'=16,'tensor'=16] {'tensor'}, use_global_device_ids=true, to_apply=%region_6.0 | all-reduce | flops 64 | bytes 512 | tf_op jit(solution)/shard_map/psum | solution.py:38
  213.5 0.7 cholesky.85
  216.6 24.0 %psum.67 = f32[16,8]{1,0:T(8,128)S(1)} all-reduce(f32[16,8]{1,0:T(8,128)S(1)} %fusion.1), channel_id=1, replica_groups=mesh['group'=16,'tensor'=16] {'tensor'}, use_global_device_ids=true, to_apply=%region_7.0 | all-reduce | flops 128 | bytes 1024 | tf_op jit(solution)/shard_map/psum | solution.py:36
  240.9 23.6 %psum.68 = f32[8,8]{0,1:T(8,128)S(1)} all-reduce(f32[8,8]{0,1:T(8,128)S(1)} %fusion.33), channel_id=1, replica_groups=mesh['group'=16,'tensor'=16] {'tensor'}, use_global_device_ids=true, to_apply=%region_8.0 | all-reduce | flops 64 | bytes 512 | tf_op jit(solution)/shard_map/psum | solution.py:38
  264.6 0.7 cholesky.96
  267.7 42.8 %psum.69 = f32[24,8]{1,0:T(8,128)S(1)} all-reduce(f32[24,8]{1,0:T(8,128)S(1)} %fusion), channel_id=1, replica_groups=mesh['group'=16,'tensor'=16] {'tensor'}, use_global_device_ids=true, to_apply=%region_9.0 | all-reduce | flops 192 | bytes 1536 | tf_op jit(solution)/shard_map/psum | solution.py:36
  310.8 26.4 %psum.70 = f32[8,8]{0,1:T(8,128)S(1)} all-reduce(f32[8,8]{0,1:T(8,128)S(1)} %fusion.34), channel_id=1, replica_groups=mesh['group'=16,'tensor'=16] {'tensor'}, use_global_device_ids=true, to_apply=%region_10.13 | all-reduce | flops 64 | bytes 512 | tf_op jit(solution)/shard_map/psum | solution.py:38
  337.4 0.7 cholesky.107
  340.3 5.9 fusion.35
  346.5 3.5 fusion.30
  350.0 3.8 convolution_convert_fusion
  353.8 234.1 %all-reduce.2.cloned.1.call-done = f32[3072,32]{0,1:T(8,128)} async-done(((f32[3072,32]{0,1:T(8,128)}), f32[3072,32]{0,1:T(8,128)}) %all-reduce.2.cloned.1.call-update) | async-done | bytes 393232 | tf_op jit(solution)/shard_map/psum | solution.py:45
  588.0 1.0 broadcast_multiply_fusion
  589.0 7.3 %subtract_bitcast_fusion = f32[1,384,3072]{2,1,0:T(8,128)} fusion(f32[384,3072]{1,0:T(8,128)} %copy-done.1, f32[384,32]{0,1:T(8,128)S(1)} %pad_maximum_fusion, f32[3072,32]{0,1:T(8,128)S(1)} %broadcast_multiply_fusion), kind=kOutput, calls=%fused_computation.1 | convolution fusion | flops 454164480 | bytes 9879552 | tf_op jit(solution)/shard_map/dot_general | solution.py:46
  596.4 53.3 %reduce-scatter.2.cloned.1.call-done = f32[24,3072]{1,0:T(8,128)} async-done(((f32[384,3072]{1,0:T(8,128)}), f32[24,3072]{1,0:T(8,128)}) %reduce-scatter.2.cloned.1.call-update) | async-done | bytes 294928 | tf_op jit(solution)/shard_map/reduce_scatter | solution.py:11
  649.7 1.6 convert_element_type.6
  (57 shorter events, 11.7 us)
Async XLA Ops:
  7.2 339.3 %copy-start = (bf16[384,3072]{1,0:T(8,128)(2,1)S(1)}, bf16[384,3072]{1,0:T(8,128)(2,1)}, u32[]{:S(2)}) copy-start(bf16[384,3072]{1,0:T(8,128)(2,1)} %param.9) | copy-start | bytes 7077892
  7.2 46.8 %all-gather.2.cloned.1.call-start = ((), (), s32[]{:S(2)}) async-start(), calls=%async_computation.2 | async-start | bytes 2506752 | tf_op jit(solution)/shard_map/all_gather | solution.py:17
  7.9 53.0 %copy-start.5 = (f32[3072,32]{0,1:T(8,128)S(1)}, f32[3072,32]{0,1:T(8,128)}, u32[]{:S(2)}) copy-start(f32[3072,32]{0,1:T(8,128)} %param.11) | copy-start | bytes 1179652
  7.9 580.0 %all-reduce.2.cloned.1.call-start = ((), (), s32[]{:S(2)}) async-start(), calls=%async_computation.3 | async-start | bytes 786432 | tf_op jit(solution)/shard_map/psum | solution.py:45
  58.7 2.2 copy-start.1
  60.9 285.6 %copy-start.2 = (bf16[384,384]{1,0:T(8,128)(2,1)S(1)}, bf16[384,384]{1,0:T(8,128)(2,1)}, u32[]{:S(2)}) copy-start(bf16[384,384]{1,0:T(8,128)(2,1)} %param.8) | copy-start | bytes 884740
  340.3 248.7 %copy-start.4 = (f32[384,32]{0,1:T(8,128)}, f32[384,32]{0,1:T(8,128)S(1)}, u32[]{:S(2)}) copy-start(f32[384,32]{0,1:T(8,128)S(1)} %pad_maximum_fusion) | copy-start | bytes 147460
  346.2 303.4 %reduce-scatter.2.cloned.1.call-start = ((), (), s32[]{:S(2)}) async-start(), calls=%async_computation.1 | async-start | bytes 5013504 | tf_op jit(solution)/shard_map/reduce_scatter | solution.py:11
  589.0 7.4 %copy-start.3 = (f32[3072,32]{0,1:T(8,128)}, f32[3072,32]{0,1:T(8,128)S(1)}, u32[]{:S(2)}) copy-start(f32[3072,32]{0,1:T(8,128)S(1)} %broadcast_multiply_fusion) | copy-start | bytes 1179652
Sparse Core Ops, SparseCore 0:
  9.8 44.1 all-gather.1
  346.4 241.5 all-reduce.1
  590.5 59.0 reduce-scatter.1
where the time goes:
time: 661 us; the launch traced here: 658 us
  waiting for transfers between devices  334 us (51%)
  blocking collectives  262 us (40%)
  matrix products  32 us (5%)
  between operations  13.9 us (2%)
  other arithmetic  13.4 us (2%)
    psum x1, waiting for transfers between devices, per_device(): right_factor = lax.psum(right_term, ('group', 'tensor')) / group_count  234 us
    psum x4, blocking collectives, per_device(): lax.psum(jnp.dot(column_block.T, column_block, precision=highest), 'tensor')  111 us
    psum x3, blocking collectives, per_device(): lax.psum(jnp.dot(earlier.T, column_block, precision=highest), 'tensor')  90.4 us
    psum x1, blocking collectives, per_device(): lax.psum(jnp.dot(moment, right_init, precision=highest), 'group')  60.5 us
    reduce_scatter x1, waiting for transfers between devices, per_device(): lax.psum_scatter(jnp.dot(attended, out_weight, preferred_element_type=jnp...  53.3 us
    all_gather x1, waiting for transfers between devices, per_device(): piece = lax.all_gather(cotangent, 'tensor', axis=0, tiled=True)  46 us
  transfers between devices with their start and end apart: 3, of which 3 were waited for; matrix products, arithmetic and copies ran while one was open for 2% of the time, Pallas kernels for 0%

commit v1 on v0

v1 whole, which is shorter than its diff:
```python
import jax
import jax.numpy as jnp
from jax import lax
from jax.experimental import pallas as pl
from jax.experimental.pallas import tpu as pltpu
from jax.sharding import PartitionSpec as P

F32, BF16 = jnp.float32, jnp.bfloat16
G, T, Z = 16, 16, 8
F, N, R = 384, 3072, 32
OWN = 24
CHIP = 48
H = N // 2
TILES = 12
NT = (((1,), (1,)), ((), ()))
TN = (((0,), (0,)), ((), ()))


def dot(a, b):
    return jnp.dot(a, b, preferred_element_type=F32)


def dot_nt(a, b):
    return lax.dot_general(a, b, NT, preferred_element_type=F32)


def split3(x):
    hi = x.astype(BF16)
    rest = x - hi.astype(F32)
    mid = rest.astype(BF16)
    lo = (rest - mid.astype(F32)).astype(BF16)
    return jnp.concatenate([hi, mid, lo], axis=0)


def fold_rows(x):
    return x[0:R] + x[R : 2 * R] + x[2 * R : 3 * R]


def fold_cols(x):
    return x[:, 0:R] + x[:, R : 2 * R] + x[:, 2 * R : 3 * R]


def comm_kernel(
    a_ref, c_ref, qt_ref, w_hbm, e_hbm,
    cf_ref, proj_ref, pt_ref, qft_ref,
    e_ref, w_ref, ehi_ref, elo_ref, qs_ref, r3_ref, re_ref, rt_ref,
    cq_all, r_send, r_in, r_all, y_send, y_in, g_all,
    st_ref, sa_in, s16_ref, sb_in, sc_all, sd_ref, sfin_ref,
    cx_in, part_ref, px_send, px_in, rsl_out, rsr_out, rsl_in, rsr_in, fin_out, fin_in,
    e_sem, w_sem, send_sem, cq_sem, r1_sem, r2_sem, y_sem, gr_sem, sb_sem, sc_sem, sd_sem,
    sib_send, sib_recv, ag_send, ag_recv, sibag_send, sibag_recv, rs_send, rs_recv,
):
    me_g, me_t = lax.axis_index("group"), lax.axis_index("tensor")
    z, core = me_t // 2, me_t % 2
    other = 1 - core
    sib = {"tensor": 2 * z + other}
    right = {"tensor": 2 * ((z + 1) % Z) + core}
    left = {"tensor": 2 * ((z + Z - 1) % Z) + core}

    def remote(src, dst, ssem, rsem, dev):
        return pltpu.make_async_remote_copy(
            src_ref=src, dst_ref=dst, send_sem=ssem, recv_sem=rsem,
            device_id=dev, device_id_type=pl.DeviceIdType.MESH,
        )

    def each_peer(count, me, body):
        def step(k, carry):
            body(k, (me + k) % count)
            return carry

        lax.fori_loop(1, count, step, 0)

    e_copies = []
    for i in range(4):
        rows = pl.ds(96 * i, 96)
        cp = pltpu.make_async_copy(e_hbm.at[rows], e_ref.at[rows], e_sem.at[i])
        cp.start()
        e_copies.append(cp)
    w_copy = pltpu.make_async_copy(w_hbm, w_ref, w_sem)
    w_copy.start()

    barrier = pltpu.get_barrier_semaphore()
    each_peer(T, me_t, lambda k, p: pl.semaphore_signal(
        barrier, inc=1, device_id={"tensor": p}, device_id_type=pl.DeviceIdType.MESH))
    each_peer(G, me_g, lambda k, p: pl.semaphore_signal(
        barrier, inc=1, device_id={"group": p}, device_id_type=pl.DeviceIdType.MESH))

    qs_ref[...] = split3(qt_ref[...])
    cq = fold_cols(dot_nt(c_ref[...], qs_ref[...]))
    cq_all[me_t] = jnp.concatenate([cq[0:8], cq[8:16], cq[16:24], jnp.zeros((8, 32), F32)], axis=1)
    pl.semaphore_wait(barrier, T + G - 2)

    def cq_copy(k, src_t, dst_t):
        return remote(cq_all.at[src_t], cq_all.at[src_t], send_sem.at[0, k], cq_sem.at[src_t], {"tensor": dst_t})

    each_peer(T, me_t, lambda k, p: cq_copy(k, me_t, p).start())

    cx_copy = remote(c_ref.at[:, pl.ds(pl.multiple_of(other * H, H), H)], cx_in, sib_send.at[0], sib_recv.at[0], sib)
    cx_copy.start()

    for i in range(4):
        rows = pl.ds(96 * i, 96)
        e_copies[i].wait()
        e = e_ref[rows, :]
        hi = e.astype(BF16)
        lo = (e - hi.astype(F32)).astype(BF16)
        ehi_ref[rows, :] = hi
        elo_ref[rows, :] = lo
        re_ref[rows, :] = fold_cols(dot_nt(hi, qs_ref[...]) + dot_nt(lo, qs_ref[...]))

    cx_copy.wait()
    mine = c_ref[:, pl.ds(pl.multiple_of(core * H, H), H)].astype(F32)
    theirs = cx_in[...].astype(F32)
    first = jnp.where(core == 0, mine, theirs)
    second = jnp.where(core == 0, theirs, mine)
    cf_ref[core, z] = jnp.concatenate([first, second], axis=0).astype(BF16)

    def ag_copy(direction, s):
        if direction == 0:
            origin, dev = (z + Z - (s - 1)) % Z, right
        else:
            origin, dev = (z + (s - 1)) % Z, left
        block = cf_ref.at[core, origin]
        if s == 4:
            block = block.at[:, pl.ds(direction * (H // 2), H // 2)]
        return remote(block, block, ag_send.at[direction, s - 1], ag_recv.at[direction, s - 1], dev)

    def sib_copy(d):
        block = cf_ref.at[core, (z + d) % Z]
        return remote(block, block, sibag_send.at[d], sibag_recv.at[d], sib)

    def ag_start(s):
        if s > 1:
            ag_copy(0, s - 1).wait_recv()
            ag_copy(1, s - 1).wait_recv()
        if s < 5:
            ag_copy(0, s).start()
            ag_copy(1, s).start()
        if s == 1:
            sib_copy(0).start()
        elif s < 5:
            sib_copy(Z - (s - 1)).start()
            sib_copy(s - 1).start()
        else:
            sib_copy(4).start()

    ag_start(1)

    each_peer(T, me_t, lambda k, p: cq_copy(k, p, me_t).wait_recv())
    x = cq_all[...]
    x = jnp.stack([x[:, :, 32 * b : 32 * b + 32] for b in range(3)], axis=1).reshape(F, R)
    rt = re_ref[...].T + fold_rows(dot(split3(x.T), a_ref[...]))
    for p in range(TILES):
        i, j = p // 3, p % 3
        r_send[p] = rt[8 * i : 8 * i + 8, 128 * j : 128 * j + 128]

    def r1_copy(k, src_g, dst_g):
        return remote(r_send.at[dst_g], r_in.at[src_g], send_sem.at[1, k], r1_sem.at[src_g], {"group": dst_g})

    def r1_start(k, p):
        @pl.when(p < TILES)
        def _():
            r1_copy(k, me_g, p).start()

    each_peer(G, me_g, r1_start)

    w_copy.wait()
    for i in range(4):
        cols = pl.ds(pl.multiple_of(other * H + i * 384, 384), 384)
        px_send[:, i * 384 : i * 384 + 384] = dot(a_ref[...], w_ref[:, cols]).astype(BF16)
    px_copy = remote(px_send, px_in, sib_send.at[1], sib_recv.at[1], sib)
    px_copy.start()
    for i in range(4):
        cols = pl.ds(pl.multiple_of(core * H + i * 384, 384), 384)
        part_ref[:, :, i * 384 : i * 384 + 384] = dot(a_ref[...], w_ref[:, cols]).reshape(Z, CHIP, 384)

    def r2_copy(k, src_g, dst_g):
        return remote(r_all.at[src_g], r_all.at[src_g], send_sem.at[2, k], r2_sem.at[src_g], {"group": dst_g})

    @pl.when(me_g < TILES)
    def _():
        each_peer(G, me_g, lambda k, p: r1_copy(k, p, me_g).wait_recv())
        r_in[me_g] = r_send[me_g]
        r_all[me_g] = jnp.sum(r_in[...], axis=0) * (1.0 / G)
        each_peer(G, me_g, lambda k, p: r2_copy(k, me_g, p).start())

    def rs_copy(direction, s):
        out, inn, dev = (rsr_out, rsl_in, right) if direction == 0 else (rsl_out, rsr_in, left)
        src, dst = out.at[s - 1], inn.at[s - 1]
        if s == 1:
            cols = pl.ds(direction * (H // 2), H // 2)
            src, dst = src.at[:, cols], dst.at[:, cols]
        return remote(src, dst, rs_send.at[direction, s - 1], rs_recv.at[direction, s - 1], dev)

    def term(d, cols=slice(None)):
        return part_ref[d, :, cols]

    def rs_start(s):
        for direction in (0, 1):
            d = (z + (5 - s)) % Z if direction == 0 else (z + Z - (5 - s)) % Z
            out, inn = (rsr_out, rsl_in) if direction == 0 else (rsl_out, rsr_in)
            if s == 1:
                cols = slice(direction * (H // 2), (direction + 1) * (H // 2))
                out[0, :, cols] = term(d, cols).astype(BF16)
            else:
                rs_copy(direction, s - 1).wait_recv()
                if s == 2:
                    got = slice(direction * (H // 2), (direction + 1) * (H // 2))
                    rest = slice((1 - direction) * (H // 2), (2 - direction) * (H // 2))
                    out[1, :, got] = (term(d, got) + inn[0, :, got].astype(F32)).astype(BF16)
                    out[1, :, rest] = term(d, rest).astype(BF16)
                else:
                    out[s - 1] = (term(d) + inn[s - 2].astype(F32)).astype(BF16)
            rs_copy(direction, s).start()

    px_copy.wait()
    part_ref[...] += px_in[...].astype(F32).reshape(Z, CHIP, H)
    rs_start(1)

    def r2_wait(k, p):
        @pl.when(p < TILES)
        def _():
            r2_copy(k, p, me_g).wait_recv()

    each_peer(G, me_g, r2_wait)
    for p in range(TILES):
        i, j = p // 3, p % 3
        rt_ref[8 * i : 8 * i + 8, 128 * j : 128 * j + 128] = r_all[p]
    r3_ref[...] = split3(rt_ref[...])

    y = fold_cols(dot_nt(a_ref[...], r3_ref[...])).reshape(T, 3, 8, R)
    y_send[...] = jnp.concatenate([y[:, 0], y[:, 1], y[:, 2], jnp.zeros((T, 8, 32), F32)], axis=2)

    def y_copy(k, src_t, dst_t):
        return remote(y_send.at[dst_t], y_in.at[src_t], send_sem.at[3, k], y_sem.at[src_t], {"tensor": dst_t})

    each_peer(T, me_t, lambda k, p: y_copy(k, me_t, p).start())

    gram = dot_nt(r3_ref[...], r3_ref[...])
    gram = fold_rows(fold_cols(gram))
    g_all[me_t] = jnp.concatenate([gram[8 * i : 8 * i + 8] for i in range(4)], axis=1)

    def g_copy(k, src_t, dst_t):
        return remote(g_all.at[src_t], g_all.at[src_t], send_sem.at[4, k], gr_sem.at[src_t], {"tensor": dst_t})

    each_peer(T, me_t, lambda k, p: g_copy(k, me_t, p).start())

    for i in range(6):
        cols = pl.ds(512 * i, 512)
        st_ref[:, cols] = fold_rows(dot(r3_ref[...], ehi_ref[:, cols]) + dot(r3_ref[...], elo_ref[:, cols]))

    ag_start(2)

    each_peer(T, me_t, lambda k, p: y_copy(k, p, me_t).wait_recv())
    y_in[me_t] = y_send[me_t]
    y_own = jnp.sum(y_in[...], axis=0)
    y_own = jnp.concatenate([y_own[:, 32 * b : 32 * b + 32] for b in range(3)], axis=0)
    y3 = split3(y_own.T)
    for i in range(6):
        cols = pl.ds(512 * i, 512)
        st_ref[:, cols] += fold_rows(dot(y3, c_ref[:, cols]))

    sa_copy = remote(st_ref.at[pl.ds(pl.multiple_of(other * 16, 16), 16)], sa_in, sib_send.at[2], sib_recv.at[2], sib)
    sa_copy.start()
    rs_start(2)
    sa_copy.wait()
    s16_ref[...] = st_ref[pl.ds(pl.multiple_of(core * 16, 16), 16), :] + sa_in[...]

    def tile(ref, p, first_row):
        rows = pl.ds(pl.multiple_of(first_row + 8 * (p // 8), 8), 8)
        return ref.at[rows, pl.ds(pl.multiple_of(384 * (p % 8), 384), 384)]

    def sb_copy(k, src_g, dst_g):
        return remote(tile(s16_ref, dst_g, 0), sb_in.at[src_g], send_sem.at[5, k], sb_sem.at[src_g], {"group": dst_g})

    each_peer(G, me_g, lambda k, p: sb_copy(k, me_g, p).start())
    ag_start(3)

    each_peer(T, me_t, lambda k, p: g_copy(k, p, me_t).wait_recv())
    gram = jnp.sum(g_all[...], axis=0)
    gram = jnp.concatenate([gram[:, 32 * i : 32 * i + 32] for i in range(4)], axis=0)
    row = lax.broadcasted_iota(jnp.int32, (R, R), 0)
    col = lax.broadcasted_iota(jnp.int32, (R, R), 1)
    m = jnp.concatenate([gram, (row == col).astype(F32)], axis=1)
    row = lax.broadcasted_iota(jnp.int32, (R, 2 * R), 0)
    for k in range(R):
        scale = lax.rsqrt(m[k : k + 1, k : k + 1])
        pivot_row = m[k : k + 1, :] * scale
        factor = m[:, k : k + 1] * scale
        m = jnp.where(row > k, m - factor * pivot_row, jnp.where(row == k, pivot_row, m))
    inverse = m[:, R : 2 * R]

    each_peer(G, me_g, lambda k, p: sb_copy(k, p, me_g).wait_recv())
    sb_in[me_g] = tile(s16_ref, me_g, 0)[...]
    sc_all[z] = jnp.sum(sb_in[...], axis=0)

    def sc_copy(k, src_z, dst_z):
        return remote(sc_all.at[src_z], sc_all.at[src_z], send_sem.at[6, k], sc_sem.at[src_z], {"tensor": 2 * dst_z + core})

    each_peer(Z, z, lambda k, p: sc_copy(k, z, p).start())
    rs_start(3)
    each_peer(Z, z, lambda k, p: sc_copy(k, p, z).wait_recv())
    sd_ref[...] = jnp.sum(sc_all[...], axis=0)
    tile(sfin_ref, me_g, core * 16)[...] = sd_ref[...]

    def sd_copy(k, src_g, dst_g):
        return remote(sd_ref, tile(sfin_ref, src_g, core * 16), send_sem.at[7, k], sd_sem.at[src_g], {"group": dst_g})

    each_peer(G, me_g, lambda k, p: sd_copy(k, me_g, p).start())
    ag_start(4)
    high = lax.Precision.HIGHEST
    pt_ref[...] = jnp.dot(inverse, rt_ref[...], precision=high, preferred_element_type=F32)
    each_peer(G, me_g, lambda k, p: sd_copy(k, p, me_g).wait_recv())
    half = sfin_ref.at[pl.ds(pl.multiple_of(core * 16, 16), 16)]
    se_copy = remote(half, half, sib_send.at[3], sib_recv.at[3], sib)
    se_copy.start()
    rs_start(4)
    ag_start(5)
    se_copy.wait()
    for i in range(6):
        cols = pl.ds(512 * i, 512)
        qft_ref[:, cols] = jnp.dot(inverse, sfin_ref[:, cols] * (1.0 / G), precision=high, preferred_element_type=F32)

    rs_copy(0, 4).wait_recv()
    rs_copy(1, 4).wait_recv()
    total = term(z) + rsl_in[3].astype(F32) + rsr_in[3].astype(F32)
    fin_out[...] = jnp.where(core == 0, total[OWN:], total[:OWN]).astype(BF16)
    fin_copy = remote(fin_out, fin_in, sib_send.at[4], sib_recv.at[4], sib)
    fin_copy.start()
    proj_ref[:, pl.ds(pl.multiple_of(core * H, H), H)] = jnp.where(core == 0, total[:OWN], total[OWN:]).astype(BF16)
    fin_copy.wait()
    proj_ref[:, pl.ds(pl.multiple_of(other * H, H), H)] = fin_in[...]

    for d in range(Z):
        sib_copy(d).wait()
    for s in range(1, 5):
        for direction in (0, 1):
            ag_copy(direction, s).wait_send()
            rs_copy(direction, s).wait_send()
    each_peer(T, me_t, lambda k, p: cq_copy(k, me_t, p).wait_send())

    def r1_wait(k, p):
        @pl.when(p < TILES)
        def _():
            r1_copy(k, me_g, p).wait_send()

    each_peer(G, me_g, r1_wait)

    @pl.when(me_g < TILES)
    def _():
        each_peer(G, me_g, lambda k, p: r2_copy(k, me_g, p).wait_send())

    each_peer(T, me_t, lambda k, p: y_copy(k, me_t, p).wait_send())
    each_peer(T, me_t, lambda k, p: g_copy(k, me_t, p).wait_send())
    each_peer(G, me_g, lambda k, p: sb_copy(k, me_g, p).wait_send())
    each_peer(Z, z, lambda k, p: sc_copy(k, z, p).wait_send())
    each_peer(G, me_g, lambda k, p: sd_copy(k, me_g, p).wait_send())


def communicate(attended, cotangent, right_init_t, out_weight, feedback):
    vmem, anywhere = pl.BlockSpec(memory_space=pltpu.VMEM), pl.BlockSpec(memory_space=pl.ANY)
    dma, v = pltpu.SemaphoreType.DMA, pltpu.VMEM
    return pl.pallas_call(
        comm_kernel,
        out_shape=(
            jax.ShapeDtypeStruct((2, Z, CHIP, H), BF16),
            jax.ShapeDtypeStruct((OWN, N), BF16),
            jax.ShapeDtypeStruct((R, F), F32),
            jax.ShapeDtypeStruct((R, N), F32),
        ),
        in_specs=[vmem, vmem, vmem, anywhere, anywhere],
        out_specs=[vmem] * 4,
        scratch_shapes=[
            v((F, N), F32), v((F, N), BF16), v((F, N), BF16), v((F, N), BF16), v((3 * R, N), BF16),
            v((3 * R, F), BF16), v((F, R), F32), v((R, F), F32),
            v((T, 8, 128), F32), v((TILES, 8, 128), F32), v((G, 8, 128), F32), v((TILES, 8, 128), F32),
            v((T, 8, 128), F32), v((T, 8, 128), F32), v((T, 8, 128), F32),
            v((R, N), F32), v((16, N), F32), v((16, N), F32), v((G, 8, 384), F32), v((Z, 8, 384), F32),
            v((8, 384), F32), v((R, N), F32),
            v((OWN, H), BF16), v((Z, CHIP, H), F32), v((F, H), BF16), v((F, H), BF16),
            v((4, CHIP, H), BF16), v((4, CHIP, H), BF16), v((4, CHIP, H), BF16), v((4, CHIP, H), BF16),
            v((OWN, H), BF16), v((OWN, H), BF16),
            dma((4,)), dma, dma((8, 16)), dma((T,)), dma((G,)), dma((G,)), dma((T,)), dma((T,)),
            dma((G,)), dma((Z,)), dma((G,)),
            dma((5,)), dma((5,)), dma((2, 4)), dma((2, 4)), dma((Z,)), dma((Z,)), dma((2, 4)), dma((2, 4)),
        ],
        compiler_params=pltpu.CompilerParams(
            collective_id=0, has_side_effects=True, vmem_limit_bytes=48 * 1024 * 1024
        ),
        name="communicate",
    )(attended, cotangent, right_init_t, out_weight, feedback)


COLS = 512


def finish_kernel(a_ref, pt_ref, c_ref, qft_ref, w_ref, e_ref, err_ref, ig_ref, lhs_ref, acc_ref):
    step = pl.program_id(0)

    @pl.when(step == 0)
    def _():
        pt = pt_ref[...]
        hi = pt.astype(BF16)
        lo = (pt - hi.astype(F32)).astype(BF16)
        stacked = jnp.concatenate([a_ref[...], -hi, -hi, -lo], axis=0)
        lhs_ref[...] = stacked.T
        acc_ref[...] = jnp.zeros_like(acc_ref)

    qt = qft_ref[...]
    hi = qt.astype(BF16)
    lo = (qt - hi.astype(F32)).astype(BF16)
    c = c_ref[0]
    err_ref[...] = e_ref[...] + dot(lhs_ref[...], jnp.concatenate([c, hi, lo, hi], axis=0))
    acc_ref[...] += dot_nt(c, w_ref[...])

    @pl.when(step == pl.num_programs(0) - 1)
    def _():
        ig_ref[...] = acc_ref[...].astype(BF16)


def finish(attended, pt, cf, qft, out_weight, feedback):
    per_half = H // COLS
    return pl.pallas_call(
        finish_kernel,
        grid=(N // COLS,),
        out_shape=(jax.ShapeDtypeStruct((F, N), F32), jax.ShapeDtypeStruct((F, F), BF16)),
        in_specs=[
            pl.BlockSpec((F, F), lambda j: (0, 0)),
            pl.BlockSpec((R, F), lambda j: (0, 0)),
            pl.BlockSpec((1, F, COLS), lambda j: (j // per_half, 0, j % per_half)),
            pl.BlockSpec((R, COLS), lambda j: (0, j)),
            pl.BlockSpec((F, COLS), lambda j: (0, j)),
            pl.BlockSpec((F, COLS), lambda j: (0, j)),
        ],
        out_specs=[pl.BlockSpec((F, COLS), lambda j: (0, j)), pl.BlockSpec((F, F), lambda j: (0, 0))],
        scratch_shapes=[pltpu.VMEM((F, F + 3 * R), BF16), pltpu.VMEM((F, F), F32)],
        compiler_params=pltpu.CompilerParams(vmem_limit_bytes=32 * 1024 * 1024),
        name="finish",
    )(attended, pt, cf, qft, out_weight, feedback)


def per_device(attended, out_weight, feedback_error, right_init, cotangent):
    feedback = feedback_error[0]
    cf, projected, pt, qft = communicate(attended, cotangent, right_init.T, out_weight, feedback)
    new_error, input_grad = finish(attended, pt, cf.reshape(2, F, H), qft, out_weight, feedback)
    return (projected, input_grad, new_error[None], pt.T, qft.T)


def solution(mesh):
    in_specs = (
        P("group", "tensor"),
        P("tensor", None),
        P("group", "tensor", None),
        P(),
        P(("group", "tensor"), None),
    )
    out_specs = (
        P(("group", "tensor"), None),
        P("group", "tensor"),
        P("group", "tensor", None),
        P("tensor", None),
        P(),
    )
    return jax.shard_map(
        per_device, mesh=mesh, in_specs=in_specs, out_specs=out_specs, check_vma=False
    )
```

time: 661 us -> 73.5 us (0.11)
  waiting for transfers between devices: 334 us -> 0 us
  blocking collectives: 262 us -> 0 us
  Pallas kernels: 0 us -> 65.7 us
  matrix products: 32 us -> 0 us
  other arithmetic: 13.4 us -> 0 us
  between operations: 13.9 us -> 0.67 us
    psum x8 -> x0, blocking collectives: 262 us -> none  [the longest x4 111 us: per_device(): lax.psum(jnp.dot(column_block.T, column_block, precision=highest), 'tensor')]
    psum x1 -> x0, waiting for transfers between devices: 234 us -> none  [per_device(): right_factor = lax.psum(right_term, ('group', 'tensor')) / group_count]
    pallas_call x0 -> x2, Pallas kernels: none -> 65.7 us  [the longest x1 59.9 us: communicate(): pl.pallas_call(comm_kernel, out_shape=(jax.ShapeDtypeStruct((2, Z, CHIP,...]
    reduce_scatter x1 -> x0, waiting for transfers between devices: 53.3 us -> none  [per_device(): lax.psum_scatter(jnp.dot(attended, out_weight, preferred_element_type=jnp...]
    all_gather x1 -> x0, waiting for transfers between devices: 46 us -> none  [per_device(): piece = lax.all_gather(cotangent, 'tensor', axis=0, tiled=True)]
    dot_general x16 -> x0, matrix products: 31.2 us -> none  [the longest x1 7.34 us: per_device(): jnp.dot(left_factor, right_factor.T, precision=highest)]
    another operation x20 -> x0, other arithmetic: 10.7 us -> none  [the longest x12 5.57 us: per_device(): block_lower = jnp.linalg.cholesky(block_gram)]
  transfers between devices with their start and end apart: 3 -> 0, of which waited for: 3 -> 0; matrix products, arithmetic and copies ran while one was open for 2% -> 0% of each run, Pallas kernels for 0% -> 0%
where the time goes in v1:
time: 73.5 us; the launch traced here: 73.4 us
  Pallas kernels  65.7 us (89%)
  local copies, waits for them, and re-layouts  7.01 us (10%)
    pallas_call x1, Pallas kernels, communicate(): pl.pallas_call(comm_kernel, out_shape=(jax.ShapeDtypeStruct((2, Z, CHIP,...  59.9 us
    unnamed x13, local copies, waits for them, and re-layouts  7.01 us
    pallas_call x1, Pallas kernels, finish(): pl.pallas_call(finish_kernel, grid=(N // COLS,), out_shape=(jax.ShapeDtyp...  5.8 us

profile of v1, /device:TPU:1, one launch (start us, length us, event | category | flops | bytes accessed | tf_op | source)
XLA Modules:
  0.0 73.4 jit_solution(6937218592729822917)
XLA Ops:
  0.6 0.0 copy-start
  0.6 0.0 copy-start.1
  0.7 1.8 %copy-done.1 = bf16[384,3072]{1,0:T(8,128)(2,1)S(1)} copy-done((bf16[384,3072]{1,0:T(8,128)(2,1)S(1)}, bf16[384,3072]{1,0:T(8,128)(2,1)}, u32[]{:S(2)}) %copy-start.1) | copy-done | bytes 2359320
  2.5 0.0 copy-start.2
  2.5 1.3 %copy-done.2 = bf16[384,384]{1,0:T(8,128)(2,1)S(1)} copy-done((bf16[384,384]{1,0:T(8,128)(2,1)S(1)}, bf16[384,384]{1,0:T(8,128)(2,1)}, u32[]{:S(2)}) %copy-start.2) | copy-done | bytes 294936
  3.7 0.0 copy-start.3
  3.7 1.0 %copy-done.3 = f32[3072,32]{0,1:T(8,128)S(1)} copy-done((f32[3072,32]{0,1:T(8,128)S(1)}, f32[3072,32]{0,1:T(8,128)}, u32[]{:S(2)}) %copy-start.3) | copy-done | bytes 393240
  4.7 0.0 copy-start.4
  4.7 0.9 %copy-done.4 = bf16[24,3072]{1,0:T(8,128)(2,1)S(1)} copy-done((bf16[24,3072]{1,0:T(8,128)(2,1)S(1)}, bf16[24,3072]{1,0:T(8,128)(2,1)}, u32[]{:S(2)}) %copy-start.4) | copy-done | bytes 147480
  5.6 59.9 %communicate.1 = (bf16[2,8,48,1536]{3,2,1,0:T(8,128)(2,1)S(1)}, bf16[24,3072]{1,0:T(8,128)(2,1)S(1)}, f32[32,384]{1,0:T(8,128)S(1)}, f32[32,3072]{1,0:T(8,128)S(1)}) custom-call(bf16[384,384]{1,0:T(8,128)(2,1)S(1)} %copy-done.2, bf16[24,3072]{1,0:T(8,128)(2,1)S(1)} %copy-done.4, f32[32,3072]{1,0:T(8,128)S(1)} %bitcast.10, bf16[384,3072]{1,0:T(8,128)(2,1)S(1)} %copy-done.1, ...), custom_call_target="tpu_custom_call" | custom-call | tf_op jit(solution)/shard_map/communicate/pallas_call | solution.py:363
  65.5 0.0 copy-done
  65.5 5.8 %finish.1 = (f32[384,3072]{1,0:T(8,128)}, bf16[384,384]{1,0:T(8,128)(2,1)}) custom-call(bf16[384,384]{1,0:T(8,128)(2,1)S(1)} %copy-done.2, f32[32,384]{1,0:T(8,128)S(1)} %get-tuple-element.12.pt_ref, bf16[2,384,1536]{2,1,0:T(8,128)(2,1)S(1)} %bitcast.8, f32[32,3072]{1,0:T(8,128)S(1)} %get-tuple-element.14.qft_ref, bf16[384,3072]{1,0:T(8,128)(2,1)S(1)} %copy-done.1, ...), custom_call_target="tpu_custom_call" | custom-call | tf_op jit(solution)/shard_map/finish/pallas_call | solution.py:423
  71.3 0.7 copy.13
  72.0 0.6 copy.14
  72.6 0.7 %copy.15 = f32[3072,32]{0,1:T(8,128)} copy(f32[3072,32]{0,1:T(8,128)S(1)} %bitcast.9) | data formatting | bytes 786432
Async XLA Ops:
  0.6 64.9 %copy-start = (f32[1,384,3072]{2,1,0:T(8,128)S(1)}, f32[1,384,3072]{2,1,0:T(8,128)}, u32[]{:S(2)}) copy-start(f32[1,384,3072]{2,1,0:T(8,128)} %param.7) | copy-start | bytes 14155780
  0.6 1.8 %copy-start.1 = (bf16[384,3072]{1,0:T(8,128)(2,1)S(1)}, bf16[384,3072]{1,0:T(8,128)(2,1)}, u32[]{:S(2)}) copy-start(bf16[384,3072]{1,0:T(8,128)(2,1)} %w_ref.1) | copy-start | bytes 7077892
  2.5 1.3 %copy-start.2 = (bf16[384,384]{1,0:T(8,128)(2,1)S(1)}, bf16[384,384]{1,0:T(8,128)(2,1)}, u32[]{:S(2)}) copy-start(bf16[384,384]{1,0:T(8,128)(2,1)} %a_ref.3) | copy-start | bytes 884740
  3.7 1.0 %copy-start.3 = (f32[3072,32]{0,1:T(8,128)S(1)}, f32[3072,32]{0,1:T(8,128)}, u32[]{:S(2)}) copy-start(f32[3072,32]{0,1:T(8,128)} %param.8) | copy-start | bytes 1179652
  4.7 0.9 %copy-start.4 = (bf16[24,3072]{1,0:T(8,128)(2,1)S(1)}, bf16[24,3072]{1,0:T(8,128)(2,1)}, u32[]{:S(2)}) copy-start(bf16[24,3072]{1,0:T(8,128)(2,1)} %c_ref.1) | copy-start | bytes 442372

commit v2 on v0

v2 whole, which is shorter than its diff:
```python
import jax
import jax.numpy as jnp
from jax import lax
from jax.experimental import pallas as pl
from jax.experimental.pallas import tpu as pltpu
from jax.sharding import PartitionSpec as P

F32, BF16 = jnp.float32, jnp.bfloat16
G, T, Z = 16, 16, 8
F, N, R = 384, 3072, 32
OWN = 24
CHIP = 48
H = N // 2
Q = H // 2
TILES = 12
NT = (((1,), (1,)), ((), ()))
TN = (((0,), (0,)), ((), ()))


def dot(a, b):
    return jnp.dot(a, b, preferred_element_type=F32)


def dot_nt(a, b):
    return lax.dot_general(a, b, NT, preferred_element_type=F32)


def split3(x):
    hi = x.astype(BF16)
    rest = x - hi.astype(F32)
    mid = rest.astype(BF16)
    lo = (rest - mid.astype(F32)).astype(BF16)
    return jnp.concatenate([hi, mid, lo], axis=0)


def fold_rows(x):
    return x[0:R] + x[R : 2 * R] + x[2 * R : 3 * R]


def hops(step, size):
    return min(step, size - step)


GROUP_OFFSETS = sorted(
    ((dx, dy) for dx in range(4) for dy in range(4) if dx or dy), key=lambda d: -hops(d[0], 4) - hops(d[1], 4)
)
TENSOR_OFFSETS = sorted(((dz, dc) for dz in range(Z) for dc in range(2) if dz or dc), key=lambda d: -hops(d[0], Z))
Z_OFFSETS = sorted(range(1, Z), key=lambda d: -hops(d, Z))


def fold_cols(x):
    return x[:, 0:R] + x[:, R : 2 * R] + x[:, 2 * R : 3 * R]


def comm_kernel(
    a_hbm, c_hbm, qt_hbm, w_hbm, e_hbm,
    m_ref, ig_ref, proj_ref, pt_ref, p3_ref, inv_ref, sfin_ref,
    a_ref, c_ref, qt_ref, w_ref, e_ref, at_ref, ehi_ref, elo_ref, qs_ref, r3_ref, re_ref, ret_ref, rt_ref,
    cq_all, r_send, r_in, r_all, g_all,
    st_ref, sa_in, s16_ref, sb_in, sc_all, sd_ref, cf_ref,
    cx_in, part_ref, px_send, px_in, rsl_out, rsr_out, rsl_in, rsr_in, fin_out, fin_in,
    load_sem, send_sem, recv_sem,
    sib_send, sib_recv, ag_send, ag_recv, sibag_send, sibag_recv, rs_send, rs_recv,
):
    me_g, me_t = lax.axis_index("group"), lax.axis_index("tensor")
    x, y = me_g // 4, me_g % 4
    z, core = me_t // 2, me_t % 2
    other = 1 - core
    sib = {"tensor": 2 * z + other}
    right = {"tensor": 2 * ((z + 1) % Z) + core}
    left = {"tensor": 2 * ((z + Z - 1) % Z) + core}
    groups = [((x + dx) % 4) * 4 + (y + dy) % 4 for dx, dy in GROUP_OFFSETS]
    tensors = [2 * ((z + dz) % Z) + (core + dc) % 2 for dz, dc in TENSOR_OFFSETS]
    chips = [(z + dz) % Z for dz in Z_OFFSETS]

    def remote(src, dst, ssem, rsem, dev):
        return pltpu.make_async_remote_copy(
            src_ref=src, dst_ref=dst, send_sem=ssem, recv_sem=rsem,
            device_id=dev, device_id_type=pl.DeviceIdType.MESH,
        )

    def send(phase, src, dst, dev):
        remote(src, dst, send_sem.at[phase], recv_sem.at[phase], dev).start()

    def arrived(phase, like):
        remote(like, like, send_sem.at[phase], recv_sem.at[phase], sib).wait_recv()

    def left_here(phase, like):
        remote(like, like, send_sem.at[phase], recv_sem.at[phase], sib).wait_send()

    def half(c):
        return pl.ds(pl.multiple_of(c * H, H), H)

    def rank_rows(c):
        return pl.ds(pl.multiple_of(c * 16, 16), 16)

    def load(i, src, dst):
        cp = pltpu.make_async_copy(src, dst, load_sem.at[i])
        cp.start()
        return cp

    qt_load, c_load = load(0, qt_hbm, qt_ref), load(1, c_hbm, c_ref)
    e_loads = [load(2 + i, e_hbm.at[pl.ds(96 * i, 96)], e_ref.at[pl.ds(96 * i, 96)]) for i in range(4)]
    a_load, w_load = load(6, a_hbm, a_ref), load(7, w_hbm, w_ref)

    barrier = pltpu.get_barrier_semaphore()
    for p in tensors:
        pl.semaphore_signal(barrier, inc=1, device_id={"tensor": p}, device_id_type=pl.DeviceIdType.MESH)
    for p in groups:
        pl.semaphore_signal(barrier, inc=1, device_id={"group": p}, device_id_type=pl.DeviceIdType.MESH)

    qt_load.wait()
    qs_ref[...] = split3(qt_ref[...])
    c_load.wait()
    cq = fold_cols(dot_nt(c_ref[...], qs_ref[...]))
    cq_all[me_t] = jnp.concatenate([cq[0:8], cq[8:16], cq[16:24], jnp.zeros((8, 32), F32)], axis=1)
    pl.semaphore_wait(barrier, T + G - 2)

    cx_copy = remote(c_ref.at[:, half(other)], cx_in, sib_send.at[0], sib_recv.at[0], sib)
    cx_copy.start()
    for p in tensors:
        send(0, cq_all.at[me_t], cq_all.at[me_t], {"tensor": p})

    def ag_copy(direction, s, q):
        origin, dev = ((z + Z - (s - 1)) % Z, right) if direction == 0 else ((z + (s - 1)) % Z, left)
        piece = cf_ref.at[core, origin, :, pl.ds(q * Q, Q)]
        return remote(piece, piece, ag_send.at[direction, s - 1, q], ag_recv.at[direction, s - 1, q], dev)

    def sib_copy(d, q):
        piece = cf_ref.at[core, (z + d) % Z, :, pl.ds(q * Q, Q)]
        return remote(piece, piece, sibag_send.at[d, q], sibag_recv.at[d, q], sib)

    def ag_step(s, q):
        if s == 0:
            ag_copy(0, 1, q).start()
            ag_copy(1, 1, q).start()
            sib_copy(0, q).start()
        elif s < 4:
            for direction in (0, 1):
                ag_copy(direction, s, q).wait_recv()
                if s < 3 or direction == q:
                    ag_copy(direction, s + 1, q).start()
            sib_copy(Z - s, q).start()
            sib_copy(s, q).start()
        else:
            ag_copy(q, 4, q).wait_recv()
            sib_copy(4, q).start()

    cx_copy.wait()
    mine = c_ref[:, half(core)].astype(F32)
    theirs = cx_in[...].astype(F32)
    first = jnp.where(core == 0, mine, theirs)
    second = jnp.where(core == 0, theirs, mine)
    cf_ref[core, z] = jnp.concatenate([first, second], axis=0).astype(BF16)
    ag_step(0, 0)
    ag_step(0, 1)

    for i in range(4):
        rows = pl.ds(96 * i, 96)
        e_loads[i].wait()
        e = e_ref[rows, :]
        hi = e.astype(BF16)
        lo = (e - hi.astype(F32)).astype(BF16)
        ehi_ref[rows, :] = hi
        elo_ref[rows, :] = lo
        re_ref[rows, :] = fold_cols(dot_nt(hi, qs_ref[...]) + dot_nt(lo, qs_ref[...]))
    ret_ref[...] = re_ref[...].T
    a_load.wait()
    at_ref[...] = a_ref[...].T

    w_load.wait()
    for i in range(4):
        cols = pl.ds(pl.multiple_of(other * H + i * 384, 384), 384)
        px_send[:, i * 384 : i * 384 + 384] = dot(a_ref[...], w_ref[:, cols]).astype(BF16)
    px_copy = remote(px_send, px_in, sib_send.at[1], sib_recv.at[1], sib)
    px_copy.start()
    ag_step(1, 0)

    arrived(0, cq_all.at[pl.ds(0, T - 1)])
    v = cq_all[...]
    v = jnp.stack([v[:, :, 32 * b : 32 * b + 32] for b in range(3)], axis=1).reshape(F, R)
    rt = ret_ref[...] + fold_rows(dot(split3(v.T), a_ref[...]))
    for p in range(TILES):
        i, j = p // 3, p % 3
        r_send[p] = rt[8 * i : 8 * i + 8, 128 * j : 128 * j + 128]

    for p in groups:
        @pl.when(p < TILES)
        def _():
            send(1, r_send.at[p], r_in.at[me_g], {"group": p})

    ag_step(1, 1)
    for i in range(4):
        cols = pl.ds(pl.multiple_of(core * H + i * 384, 384), 384)
        part_ref[:, :, i * 384 : i * 384 + 384] = dot(a_ref[...], w_ref[:, cols]).reshape(Z, CHIP, 384)

    def rs_copy(direction, s):
        out, inn, dev = (rsr_out, rsl_in, right) if direction == 0 else (rsl_out, rsr_in, left)
        src, dst = out.at[s - 1], inn.at[s - 1]
        if s == 1:
            cols = pl.ds(direction * Q, Q)
            src, dst = src.at[:, cols], dst.at[:, cols]
        return remote(src, dst, rs_send.at[direction, s - 1], rs_recv.at[direction, s - 1], dev)

    def rs_step(s):
        for direction in (0, 1):
            d = (z + (5 - s)) % Z if direction == 0 else (z + Z - (5 - s)) % Z
            out, inn = (rsr_out, rsl_in) if direction == 0 else (rsl_out, rsr_in)
            got, rest = slice(direction * Q, direction * Q + Q), slice((1 - direction) * Q, (1 - direction) * Q + Q)
            if s == 1:
                out[0, :, got] = part_ref[d, :, got].astype(BF16)
            else:
                rs_copy(direction, s - 1).wait_recv()
                if s == 2:
                    out[1, :, got] = (part_ref[d, :, got] + inn[0, :, got].astype(F32)).astype(BF16)
                    out[1, :, rest] = part_ref[d, :, rest].astype(BF16)
                else:
                    out[s - 1] = (part_ref[d] + inn[s - 2].astype(F32)).astype(BF16)
            rs_copy(direction, s).start()

    px_copy.wait()
    part_ref[...] += px_in[...].astype(F32).reshape(Z, CHIP, H)
    ag_step(2, 0)

    @pl.when(me_g < TILES)
    def _():
        arrived(1, r_in.at[pl.ds(0, G - 1)])
        r_in[me_g] = r_send[me_g]
        r_all[me_g] = jnp.sum(r_in[...], axis=0) * (1.0 / G)
        for p in groups:
            send(2, r_all.at[me_g], r_all.at[me_g], {"group": p})

    ag_step(2, 1)
    rs_step(1)
    ag_step(3, 0)
    ag_step(3, 1)

    @pl.when(me_g < TILES)
    def _():
        arrived(2, r_all.at[pl.ds(0, TILES - 1)])

    @pl.when(me_g >= TILES)
    def _():
        arrived(2, r_all)

    for p in range(TILES):
        i, j = p // 3, p % 3
        rt_ref[8 * i : 8 * i + 8, 128 * j : 128 * j + 128] = r_all[p]
    r3_ref[...] = split3(rt_ref[...])

    y3 = split3(fold_rows(dot(r3_ref[...], at_ref[...])))
    for i in range(6):
        cols = pl.ds(512 * i, 512)
        st_ref[:, cols] = fold_rows(dot(r3_ref[...], ehi_ref[:, cols]) + dot(r3_ref[...], elo_ref[:, cols]))
    gram = fold_rows(fold_cols(dot_nt(r3_ref[...], r3_ref[...])))
    g_all[me_t] = jnp.concatenate([gram[8 * i : 8 * i + 8] for i in range(4)], axis=1)
    for p in tensors:
        send(3, g_all.at[me_t], g_all.at[me_t], {"tensor": p})
    ag_step(4, 0)
    ag_step(4, 1)

    def add_cotangent(c):
        for i in range(3):
            cols = pl.ds(pl.multiple_of(c * H + 512 * i, 512), 512)
            block = cf_ref[c, :, :, 512 * i : 512 * i + 512].reshape(F, 512)
            st_ref[:, cols] += fold_rows(dot(y3, block))

    def sa_copy(n, c):
        return remote(
            st_ref.at[rank_rows(other), half(c)], sa_in.at[:, half(c)], sib_send.at[2 + n], sib_recv.at[2 + n], sib
        )

    add_cotangent(core)
    sa_copy(0, core).start()
    for d in range(Z):
        for q in (0, 1):
            sib_copy(d, q).wait()
    add_cotangent(other)
    sa_copy(1, other).start()
    sa_copy(0, core).wait_send()
    sa_copy(0, other).wait_recv()
    sa_copy(1, other).wait_send()
    sa_copy(1, core).wait_recv()
    s16_ref[...] = st_ref[rank_rows(core), :] + sa_in[...]

    def tile(ref, p, first_row):
        rows = pl.ds(pl.multiple_of(first_row + 8 * (p // 8), 8), 8)
        return ref.at[rows, pl.ds(pl.multiple_of(384 * (p % 8), 384), 384)]

    for p in groups:
        send(4, tile(s16_ref, p, 0), sb_in.at[me_g], {"group": p})
    rs_step(2)

    for c in (0, 1):
        for i in range(3):
            cols = pl.ds(c * H + 512 * i, 512)
            m_ref[:, cols] = e_ref[:, cols] + dot(at_ref[...], cf_ref[c, :, :, 512 * i : 512 * i + 512].reshape(F, 512))

    arrived(4, sb_in.at[pl.ds(0, G - 1)])
    sb_in[me_g] = tile(s16_ref, me_g, 0)[...]
    sc_all[z] = jnp.sum(sb_in[...], axis=0)
    for p in chips:
        send(5, sc_all.at[z], sc_all.at[z], {"tensor": 2 * p + core})
    rs_step(3)

    arrived(3, g_all.at[pl.ds(0, T - 1)])
    gram = jnp.sum(g_all[...], axis=0)
    gram = jnp.concatenate([gram[:, 32 * i : 32 * i + 32] for i in range(4)], axis=0)
    row = lax.broadcasted_iota(jnp.int32, (R, R), 0)
    col = lax.broadcasted_iota(jnp.int32, (R, R), 1)
    both = jnp.concatenate([gram, (row == col).astype(F32)], axis=1)
    row = lax.broadcasted_iota(jnp.int32, (R, 2 * R), 0)
    for k in range(R):
        scale = lax.rsqrt(both[k : k + 1, k : k + 1])
        pivot_row = both[k : k + 1, :] * scale
        factor = both[:, k : k + 1] * scale
        both = jnp.where(row > k, both - factor * pivot_row, jnp.where(row == k, pivot_row, both))
    inv_ref[...] = both[:, R : 2 * R]

    arrived(5, sc_all.at[pl.ds(0, Z - 1)])
    sd_ref[...] = jnp.sum(sc_all[...], axis=0)
    tile(sfin_ref, me_g, core * 16)[...] = sd_ref[...]
    for p in groups:
        send(6, sd_ref, tile(sfin_ref, me_g, core * 16), {"group": p})

    pt = jnp.dot(inv_ref[...], rt_ref[...], precision=lax.Precision.HIGHEST, preferred_element_type=F32)
    pt_ref[...] = pt
    hi = pt.astype(BF16)
    lo = (pt - hi.astype(F32)).astype(BF16)
    p3_ref[...] = -jnp.concatenate([hi, hi, lo], axis=0)
    rs_step(4)
    back = dot_nt(cf_ref[0].reshape(F, H), w_ref[:, :H]) + dot_nt(cf_ref[1].reshape(F, H), w_ref[:, H:])
    ig_ref[...] = back.astype(BF16)

    arrived(6, sb_in.at[pl.ds(0, G - 1)])
    mine = sfin_ref.at[rank_rows(core)]
    se_copy = remote(mine, mine, sib_send.at[4], sib_recv.at[4], sib)
    se_copy.start()

    rs_copy(0, 4).wait_recv()
    rs_copy(1, 4).wait_recv()
    total = part_ref[z] + rsl_in[3].astype(F32) + rsr_in[3].astype(F32)
    fin_out[...] = jnp.where(core == 0, total[OWN:], total[:OWN]).astype(BF16)
    fin_copy = remote(fin_out, fin_in, sib_send.at[5], sib_recv.at[5], sib)
    fin_copy.start()
    proj_ref[:, half(core)] = jnp.where(core == 0, total[:OWN], total[OWN:]).astype(BF16)
    se_copy.wait()
    fin_copy.wait()
    proj_ref[:, half(other)] = fin_in[...]

    for q in (0, 1):
        for s in range(1, 5):
            for direction in (0, 1):
                if s < 4 or direction == q:
                    ag_copy(direction, s, q).wait_send()
    for s in range(1, 5):
        for direction in (0, 1):
            rs_copy(direction, s).wait_send()
    left_here(0, cq_all.at[pl.ds(0, T - 1)])

    @pl.when(me_g < TILES)
    def _():
        left_here(1, r_in.at[pl.ds(0, TILES - 1)])
        left_here(2, r_in.at[pl.ds(0, G - 1)])

    @pl.when(me_g >= TILES)
    def _():
        left_here(1, r_in.at[pl.ds(0, TILES)])

    left_here(3, g_all.at[pl.ds(0, T - 1)])
    left_here(4, sb_in.at[pl.ds(0, G - 1)])
    left_here(5, sc_all.at[pl.ds(0, Z - 1)])
    left_here(6, sb_in.at[pl.ds(0, G - 1)])


def communicate(attended, cotangent, right_init_t, out_weight, feedback):
    vmem, hbm = pl.BlockSpec(memory_space=pltpu.VMEM), pl.BlockSpec(memory_space=pltpu.HBM)
    dma, v = pltpu.SemaphoreType.DMA, pltpu.VMEM
    return pl.pallas_call(
        comm_kernel,
        out_shape=(
            jax.ShapeDtypeStruct((F, N), F32),
            jax.ShapeDtypeStruct((F, F), BF16),
            jax.ShapeDtypeStruct((OWN, N), BF16),
            jax.ShapeDtypeStruct((R, F), F32),
            jax.ShapeDtypeStruct((3 * R, F), BF16),
            jax.ShapeDtypeStruct((R, R), F32),
            jax.ShapeDtypeStruct((R, N), F32),
        ),
        in_specs=[hbm] * 5,
        out_specs=[vmem] * 7,
        scratch_shapes=[
            v((F, F), BF16), v((OWN, N), BF16), v((R, N), F32), v((F, N), BF16), v((F, N), F32),
            v((F, F), BF16), v((F, N), BF16), v((F, N), BF16), v((3 * R, N), BF16),
            v((3 * R, F), BF16), v((F, R), F32), v((R, F), F32), v((R, F), F32),
            v((T, 8, 128), F32), v((TILES, 8, 128), F32), v((G, 8, 128), F32), v((TILES, 8, 128), F32), v((T, 8, 128), F32),
            v((R, N), F32), v((16, N), F32), v((16, N), F32), v((G, 8, 384), F32), v((Z, 8, 384), F32),
            v((8, 384), F32), v((2, Z, CHIP, H), BF16),
            v((OWN, H), BF16), v((Z, CHIP, H), F32), v((F, H), BF16), v((F, H), BF16),
            v((4, CHIP, H), BF16), v((4, CHIP, H), BF16), v((4, CHIP, H), BF16), v((4, CHIP, H), BF16),
            v((OWN, H), BF16), v((OWN, H), BF16),
            dma((8,)), dma((7,)), dma((7,)),
            dma((6,)), dma((6,)), dma((2, 4, 2)), dma((2, 4, 2)), dma((Z, 2)), dma((Z, 2)), dma((2, 4)), dma((2, 4)),
        ],
        compiler_params=pltpu.CompilerParams(
            collective_id=0, has_side_effects=True, vmem_limit_bytes=40 * 1024 * 1024
        ),
        name="communicate",
    )(attended, cotangent, right_init_t, out_weight, feedback)


COLS = 512


def finish_kernel(
    m_ref, ig_ref, proj_ref, pt_ref, p3_ref, inv_ref, s_ref,
    err_hbm, ig_hbm, proj_hbm, pt_hbm, qt_hbm,
    err_ref, qt_ref, sem, err_sem,
):
    copies = [
        pltpu.make_async_copy(ig_ref, ig_hbm, sem.at[0]),
        pltpu.make_async_copy(proj_ref, proj_hbm, sem.at[1]),
        pltpu.make_async_copy(pt_ref, pt_hbm, sem.at[2]),
    ]
    for cp in copies:
        cp.start()
    p3 = p3_ref[...].T
    for i in range(N // COLS):
        cols = pl.ds(i * COLS, COLS)
        qt = jnp.dot(inv_ref[...], s_ref[:, cols] * (1.0 / G), precision=lax.Precision.HIGHEST, preferred_element_type=F32)
        qt_ref[:, cols] = qt
        hi = qt.astype(BF16)
        lo = (qt - hi.astype(F32)).astype(BF16)
        err_ref[i] = m_ref[:, cols] + dot(p3, jnp.concatenate([hi, lo, hi], axis=0))
        cp = pltpu.make_async_copy(err_ref.at[i], err_hbm.at[:, cols], err_sem.at[i])
        cp.start()
        copies.append(cp)
    cp = pltpu.make_async_copy(qt_ref, qt_hbm, sem.at[3])
    cp.start()
    copies.append(cp)
    for cp in copies:
        cp.wait()


def finish(m, ig, proj, pt, p3, inv, s):
    vmem, hbm = pl.BlockSpec(memory_space=pltpu.VMEM), pl.BlockSpec(memory_space=pltpu.HBM)
    return pl.pallas_call(
        finish_kernel,
        out_shape=(
            jax.ShapeDtypeStruct((F, N), F32),
            jax.ShapeDtypeStruct((F, F), BF16),
            jax.ShapeDtypeStruct((OWN, N), BF16),
            jax.ShapeDtypeStruct((R, F), F32),
            jax.ShapeDtypeStruct((R, N), F32),
        ),
        in_specs=[vmem] * 7,
        out_specs=[hbm] * 5,
        scratch_shapes=[
            pltpu.VMEM((N // COLS, F, COLS), F32), pltpu.VMEM((R, N), F32),
            pltpu.SemaphoreType.DMA((4,)), pltpu.SemaphoreType.DMA((N // COLS,)),
        ],
        compiler_params=pltpu.CompilerParams(vmem_limit_bytes=32 * 1024 * 1024),
        name="finish",
    )(m, ig, proj, pt, p3, inv, s)


def per_device(attended, out_weight, feedback_error, right_init, cotangent):
    operands = (attended, cotangent, right_init.T, out_weight, feedback_error[0])
    parts = communicate(*(pltpu.with_memory_space_constraint(x, pltpu.HBM) for x in operands))
    new_error, input_grad, projected, pt, qt = finish(*parts)
    return (projected, input_grad, new_error[None], pt.T, qt.T)


def solution(mesh):
    in_specs = (
        P("group", "tensor"),
        P("tensor", None),
        P("group", "tensor", None),
        P(),
        P(("group", "tensor"), None),
    )
    out_specs = (
        P(("group", "tensor"), None),
        P("group", "tensor"),
        P("group", "tensor", None),
        P("tensor", None),
        P(),
    )
    return jax.shard_map(
        per_device, mesh=mesh, in_specs=in_specs, out_specs=out_specs, check_vma=False
    )
```

time: 661 us -> 56 us (0.08)
  waiting for transfers between devices: 334 us -> 0 us
  blocking collectives: 262 us -> 0 us
  Pallas kernels: 0 us -> 55.3 us
  matrix products: 32 us -> 0 us
  other arithmetic: 13.4 us -> 0 us
  between operations: 13.9 us -> 0.64 us
    psum x8 -> x0, blocking collectives: 262 us -> none  [the longest x4 111 us: per_device(): lax.psum(jnp.dot(column_block.T, column_block, precision=highest), 'tensor')]
    psum x1 -> x0, waiting for transfers between devices: 234 us -> none  [per_device(): right_factor = lax.psum(right_term, ('group', 'tensor')) / group_count]
    pallas_call x0 -> x2, Pallas kernels: none -> 55.3 us  [the longest x1 52.1 us: communicate(): pl.pallas_call(comm_kernel, out_shape=(jax.ShapeDtypeStruct((F, N), F32),...]
    reduce_scatter x1 -> x0, waiting for transfers between devices: 53.3 us -> none  [per_device(): lax.psum_scatter(jnp.dot(attended, out_weight, preferred_element_type=jnp...]
    all_gather x1 -> x0, waiting for transfers between devices: 46 us -> none  [per_device(): piece = lax.all_gather(cotangent, 'tensor', axis=0, tiled=True)]
    dot_general x16 -> x0, matrix products: 31.2 us -> none  [the longest x1 7.34 us: per_device(): jnp.dot(left_factor, right_factor.T, precision=highest)]
    another operation x20 -> x0, other arithmetic: 10.7 us -> none  [the longest x12 5.57 us: per_device(): block_lower = jnp.linalg.cholesky(block_gram)]
  transfers between devices with their start and end apart: 3 -> 0, of which waited for: 3 -> 0; matrix products, arithmetic and copies ran while one was open for 2% -> 0% of each run, Pallas kernels for 0% -> 0%
where the time goes in v2:
time: 56 us; the launch traced here: 55.9 us
  Pallas kernels  55.3 us (99%)
  between operations  0.64 us (1%)
    pallas_call x1, Pallas kernels, communicate(): pl.pallas_call(comm_kernel, out_shape=(jax.ShapeDtypeStruct((F, N), F32),...  52.1 us
    pallas_call x1, Pallas kernels, finish(): pl.pallas_call(finish_kernel, out_shape=(jax.ShapeDtypeStruct((F, N), F32...  3.12 us

profile of v2, /device:TPU:1, one launch (start us, length us, event | category | flops | bytes accessed | tf_op | source)
XLA Modules:
  0.0 55.9 jit_solution(5818511202006866249)
XLA Ops:
  0.6 52.1 %communicate.1 = (f32[384,3072]{1,0:T(8,128)S(1)}, bf16[384,384]{1,0:T(8,128)(2,1)S(1)}, bf16[24,3072]{1,0:T(8,128)(2,1)S(1)}, f32[32,384]{1,0:T(8,128)S(1)}, bf...) custom-call(bf16[384,384]{1,0:T(8,128)(2,1)} %a_hbm.1, bf16[24,3072]{1,0:T(8,128)(2,1)} %c_hbm.1, ...), custom_call_target="tpu_custom_call" | custom-call | tf_op jit(solution)/shard_map/communicate/pallas_call | solution.py:379
  52.8 3.1 %finish.1 = (f32[384,3072]{1,0:T(8,128)}, bf16[384,384]{1,0:T(8,128)(2,1)}, bf16[24,3072]{1,0:T(8,128)(2,1)}, f32[32,384]{1,0:T(8,128)}, f32[32,3072]{1,0:T(8,128)}) custom-call(f32[384,3072]{1,0:T(8,128)S(1)} %get-tuple-element.17.m_ref, bf16[384,384]{1,0:T(8,128)(2,1)S(1)} %get-tuple-element.18.ig_ref, bf16[24,3072]{1,0:T(8,128)(2,1)S(1)} %get-tuple-element.19.proj_ref, ...), custom_call_target="tpu_custom_call" | custom-call | tf_op jit(solution)/shard_map/finish/pallas_call | solution.py:447

commit v3 on v2

--- a/solution.py
+++ b/solution.py
@@ -12,6 +12,8 @@
 CHIP = 48
 H = N // 2
 Q = H // 2
+PIECES = 4
+PIECE = H // PIECES
 TILES = 12
 NT = (((1,), (1,)), ((), ()))
 TN = (((0,), (0,)), ((), ()))
@@ -57,10 +59,10 @@
     m_ref, ig_ref, proj_ref, pt_ref, p3_ref, inv_ref, sfin_ref,
     a_ref, c_ref, qt_ref, w_ref, e_ref, at_ref, ehi_ref, elo_ref, qs_ref, r3_ref, re_ref, ret_ref, rt_ref,
     cq_all, r_send, r_in, r_all, g_all,
-    st_ref, sa_in, s16_ref, sb_in, sc_all, sd_ref, cf_ref,
-    cx_in, part_ref, px_send, px_in, rsl_out, rsr_out, rsl_in, rsr_in, fin_out, fin_in,
+    y_ref, y_in, st_ref, sa_in, s16_ref, sb_in, sc_all, sd_ref, cf_ref,
+    land, cx_in, part_ref, px_send, px_in, rsl_out, rsr_out, rsl_in, rsr_in, fin_out, fin_in,
     load_sem, send_sem, recv_sem,
-    sib_send, sib_recv, ag_send, ag_recv, sibag_send, sibag_recv, rs_send, rs_recv,
+    sib_send, sib_recv, land_send, land_recv, ag_send, ag_recv, sibag_send, sibag_recv, rs_send, rs_recv,
 ):
     me_g, me_t = lax.axis_index("group"), lax.axis_index("tensor")
     x, y = me_g // 4, me_g % 4
@@ -91,9 +93,6 @@
     def half(c):
         return pl.ds(pl.multiple_of(c * H, H), H)
 
-    def rank_rows(c):
-        return pl.ds(pl.multiple_of(c * 16, 16), 16)
-
     def load(i, src, dst):
         cp = pltpu.make_async_copy(src, dst, load_sem.at[i])
         cp.start()
@@ -116,44 +115,61 @@
     cq_all[me_t] = jnp.concatenate([cq[0:8], cq[8:16], cq[16:24], jnp.zeros((8, 32), F32)], axis=1)
     pl.semaphore_wait(barrier, T + G - 2)
 
-    cx_copy = remote(c_ref.at[:, half(other)], cx_in, sib_send.at[0], sib_recv.at[0], sib)
-    cx_copy.start()
     for p in tensors:
         send(0, cq_all.at[me_t], cq_all.at[me_t], {"tensor": p})
 
-    def ag_copy(direction, s, q):
-        origin, dev = ((z + Z - (s - 1)) % Z, right) if direction == 0 else ((z + (s - 1)) % Z, left)
-        piece = cf_ref.at[core, origin, :, pl.ds(q * Q, Q)]
-        return remote(piece, piece, ag_send.at[direction, s - 1, q], ag_recv.at[direction, s - 1, q], dev)
+    def land_copy(direction, h, k):
+        to = (z + 1) % Z if direction == 0 else (z + Z - 1) % Z
+        return remote(
+            c_ref.at[:, pl.ds(h * H + k * PIECE, PIECE)], land.at[direction, core, :, pl.ds(k * PIECE, PIECE)],
+            land_send.at[direction, h, k], land_recv.at[direction, core, k], {"tensor": 2 * to + h},
+        )
+
+    def land_wait(direction, c, k):
+        piece = land.at[direction, c, :, pl.ds(k * PIECE, PIECE)]
+        remote(piece, piece, land_send.at[direction, c, k], land_recv.at[direction, c, k], sib).wait_recv()
+
+    def origin(direction, s):
+        return (z + Z - s) % Z if direction == 0 else (z + s) % Z
+
+    def ag_copy(direction, s, k):
+        piece = cf_ref.at[core, origin(direction, s - 1), :, pl.ds(k * PIECE, PIECE)]
+        dev = right if direction == 0 else left
+        return remote(piece, piece, ag_send.at[direction, s - 2, k], ag_recv.at[direction, s - 2, k], dev)
 
     def sib_copy(d, q):
         piece = cf_ref.at[core, (z + d) % Z, :, pl.ds(q * Q, Q)]
         return remote(piece, piece, sibag_send.at[d, q], sibag_recv.at[d, q], sib)
 
-    def ag_step(s, q):
-        if s == 0:
-            ag_copy(0, 1, q).start()
-            ag_copy(1, 1, q).start()
-            sib_copy(0, q).start()
-        elif s < 4:
-            for direction in (0, 1):
-                ag_copy(direction, s, q).wait_recv()
-                if s < 3 or direction == q:
-                    ag_copy(direction, s + 1, q).start()
-            sib_copy(Z - s, q).start()
-            sib_copy(s, q).start()
-        else:
-            ag_copy(q, 4, q).wait_recv()
-            sib_copy(4, q).start()
-
-    cx_copy.wait()
-    mine = c_ref[:, half(core)].astype(F32)
-    theirs = cx_in[...].astype(F32)
-    first = jnp.where(core == 0, mine, theirs)
-    second = jnp.where(core == 0, theirs, mine)
-    cf_ref[core, z] = jnp.concatenate([first, second], axis=0).astype(BF16)
-    ag_step(0, 0)
-    ag_step(0, 1)
+    def goes_round(direction, k):
+        return direction == k // (PIECES // 2)
+
+    def ag_step(s, k):
+        for direction in (0, 1):
+            if s == 1:
+                cols = slice(k * PIECE, (k + 1) * PIECE)
+                rows = []
+                for c in (0, 1):
+                    land_wait(direction, c, k)
+                    rows.append(land[direction, c, :, cols].astype(F32))
+                cf_ref[core, origin(direction, 1), :, cols] = jnp.concatenate(rows, axis=0).astype(BF16)
+            elif s < 4 or goes_round(direction, k):
+                ag_copy(direction, s, k).wait_recv()
+            if s < 3 or (s == 3 and goes_round(direction, k)):
+                ag_copy(direction, s + 1, k).start()
+        if k % 2 == 1:
+            for d in sorted({s, Z - s}):
+                sib_copy(d, k // 2).start()
+
+    def land_start(k):
+        for direction in (0, 1):
+            for h in (0, 1):
+                land_copy(direction, h, k).start()
+
+    land_start(0)
+    land_start(1)
+    cx_copy = remote(c_ref, cx_in, sib_send.at[0], sib_recv.at[0], sib)
+    cx_copy.start()
 
     for i in range(4):
         rows = pl.ds(96 * i, 96)
@@ -164,6 +180,8 @@
         ehi_ref[rows, :] = hi
         elo_ref[rows, :] = lo
         re_ref[rows, :] = fold_cols(dot_nt(hi, qs_ref[...]) + dot_nt(lo, qs_ref[...]))
+        if i > 1:
+            land_start(i)
     ret_ref[...] = re_ref[...].T
     a_load.wait()
     at_ref[...] = a_ref[...].T
@@ -190,37 +208,39 @@
             send(1, r_send.at[p], r_in.at[me_g], {"group": p})
 
     ag_step(1, 1)
+    ag_step(1, 2)
+    ag_step(1, 3)
+    cx_copy.wait()
+    mine, theirs = c_ref[...].astype(F32), cx_in[...].astype(F32)
+    block = jnp.concatenate([jnp.where(core == 0, mine, theirs), jnp.where(core == 0, theirs, mine)], axis=0)
+    for c in (0, 1):
+        cf_ref[c, z] = block[:, c * H : (c + 1) * H].astype(BF16)
     for i in range(4):
         cols = pl.ds(pl.multiple_of(core * H + i * 384, 384), 384)
         part_ref[:, :, i * 384 : i * 384 + 384] = dot(a_ref[...], w_ref[:, cols]).reshape(Z, CHIP, 384)
 
-    def rs_copy(direction, s):
+    def rs_copy(direction, s, q):
         out, inn, dev = (rsr_out, rsl_in, right) if direction == 0 else (rsl_out, rsr_in, left)
-        src, dst = out.at[s - 1], inn.at[s - 1]
-        if s == 1:
-            cols = pl.ds(direction * Q, Q)
-            src, dst = src.at[:, cols], dst.at[:, cols]
-        return remote(src, dst, rs_send.at[direction, s - 1], rs_recv.at[direction, s - 1], dev)
-
-    def rs_step(s):
+        cols = pl.ds(q * Q, Q)
+        return remote(
+            out.at[s - 1, :, cols], inn.at[s - 1, :, cols], rs_send.at[direction, s - 1, q], rs_recv.at[direction, s - 1, q], dev
+        )
+
+    def rs_step(s, same):
         for direction in (0, 1):
+            q = direction if same else 1 - direction
             d = (z + (5 - s)) % Z if direction == 0 else (z + Z - (5 - s)) % Z
             out, inn = (rsr_out, rsl_in) if direction == 0 else (rsl_out, rsr_in)
-            got, rest = slice(direction * Q, direction * Q + Q), slice((1 - direction) * Q, (1 - direction) * Q + Q)
-            if s == 1:
-                out[0, :, got] = part_ref[d, :, got].astype(BF16)
+            cols = slice(q * Q, q * Q + Q)
+            if s == (1 if same else 2):
+                out[s - 1, :, cols] = part_ref[d, :, cols].astype(BF16)
             else:
-                rs_copy(direction, s - 1).wait_recv()
-                if s == 2:
-                    out[1, :, got] = (part_ref[d, :, got] + inn[0, :, got].astype(F32)).astype(BF16)
-                    out[1, :, rest] = part_ref[d, :, rest].astype(BF16)
-                else:
-                    out[s - 1] = (part_ref[d] + inn[s - 2].astype(F32)).astype(BF16)
-            rs_copy(direction, s).start()
-
-    px_copy.wait()
-    part_ref[...] += px_in[...].astype(F32).reshape(Z, CHIP, H)
+                rs_copy(direction, s - 1, q).wait_recv()
+                out[s - 1, :, cols] = (part_ref[d, :, cols] + inn[s - 2, :, cols].astype(F32)).astype(BF16)
+            rs_copy(direction, s, q).start()
+
     ag_step(2, 0)
+    ag_step(2, 1)
 
     @pl.when(me_g < TILES)
     def _():
@@ -230,10 +250,14 @@
         for p in groups:
             send(2, r_all.at[me_g], r_all.at[me_g], {"group": p})
 
-    ag_step(2, 1)
-    rs_step(1)
-    ag_step(3, 0)
-    ag_step(3, 1)
+    ag_step(2, 2)
+    ag_step(2, 3)
+    px_copy.wait_recv()
+    part_ref[...] += px_in[...].astype(F32).reshape(Z, CHIP, H)
+    for k in range(PIECES):
+        ag_step(3, k)
+    rs_step(1, True)
+    rs_step(2, False)
 
     @pl.when(me_g < TILES)
     def _():
@@ -248,49 +272,45 @@
         rt_ref[8 * i : 8 * i + 8, 128 * j : 128 * j + 128] = r_all[p]
     r3_ref[...] = split3(rt_ref[...])
 
-    y3 = split3(fold_rows(dot(r3_ref[...], at_ref[...])))
-    for i in range(6):
-        cols = pl.ds(512 * i, 512)
-        st_ref[:, cols] = fold_rows(dot(r3_ref[...], ehi_ref[:, cols]) + dot(r3_ref[...], elo_ref[:, cols]))
+    y_ref[...] = fold_rows(dot(r3_ref[...], at_ref[...]))
+    y_copy = remote(y_ref, y_in, sib_send.at[2], sib_recv.at[2], sib)
+    y_copy.start()
+
+    def feedback_term(c):
+        for i in range(3):
+            cols = pl.ds(pl.multiple_of(c * H + 512 * i, 512), 512)
+            st_ref[:, cols] = fold_rows(dot(r3_ref[...], ehi_ref[:, cols]) + dot(r3_ref[...], elo_ref[:, cols]))
+
+    feedback_term(other)
+    sa_copy = remote(st_ref.at[:, half(other)], sa_in, sib_send.at[3], sib_recv.at[3], sib)
+    sa_copy.start()
+    feedback_term(core)
+    for k in range(PIECES):
+        ag_step(4, k)
+    y_copy.wait_recv()
+    y3 = split3(y_ref[...] + y_in[...])
+    sa_copy.wait_recv()
+    for i in range(3):
+        cols = slice(512 * i, 512 * i + 512)
+        part = st_ref[:, pl.ds(pl.multiple_of(core * H + 512 * i, 512), 512)] + sa_in[:, cols]
+        s16_ref[:, cols] = part + fold_rows(dot(y3, cf_ref[core, :, :, cols].reshape(F, 512)))
+
+    def tile(ref, p, first_col):
+        rows = pl.ds(pl.multiple_of(8 * (p // 4), 8), 8)
+        return ref.at[rows, pl.ds(pl.multiple_of(first_col + 384 * (p % 4), 384), 384)]
+
+    for p in groups:
+        send(4, tile(s16_ref, p, 0), sb_in.at[me_g], {"group": p})
     gram = fold_rows(fold_cols(dot_nt(r3_ref[...], r3_ref[...])))
     g_all[me_t] = jnp.concatenate([gram[8 * i : 8 * i + 8] for i in range(4)], axis=1)
     for p in tensors:
         send(3, g_all.at[me_t], g_all.at[me_t], {"tensor": p})
-    ag_step(4, 0)
-    ag_step(4, 1)
-
-    def add_cotangent(c):
-        for i in range(3):
-            cols = pl.ds(pl.multiple_of(c * H + 512 * i, 512), 512)
-            block = cf_ref[c, :, :, 512 * i : 512 * i + 512].reshape(F, 512)
-            st_ref[:, cols] += fold_rows(dot(y3, block))
-
-    def sa_copy(n, c):
-        return remote(
-            st_ref.at[rank_rows(other), half(c)], sa_in.at[:, half(c)], sib_send.at[2 + n], sib_recv.at[2 + n], sib
-        )
-
-    add_cotangent(core)
-    sa_copy(0, core).start()
-    for d in range(Z):
+    rs_step(2, True)
+    rs_step(3, False)
+
+    for d in range(1, Z):
         for q in (0, 1):
-            sib_copy(d, q).wait()
-    add_cotangent(other)
-    sa_copy(1, other).start()
-    sa_copy(0, core).wait_send()
-    sa_copy(0, other).wait_recv()
-    sa_copy(1, other).wait_send()
-    sa_copy(1, core).wait_recv()
-    s16_ref[...] = st_ref[rank_rows(core), :] + sa_in[...]
-
-    def tile(ref, p, first_row):
-        rows = pl.ds(pl.multiple_of(first_row + 8 * (p // 8), 8), 8)
-        return ref.at[rows, pl.ds(pl.multiple_of(384 * (p % 8), 384), 384)]
-
-    for p in groups:
-        send(4, tile(s16_ref, p, 0), sb_in.at[me_g], {"group": p})
-    rs_step(2)
-
+            sib_copy(d, q).wait_recv()
     for c in (0, 1):
         for i in range(3):
             cols = pl.ds(c * H + 512 * i, 512)
@@ -301,7 +321,8 @@
     sc_all[z] = jnp.sum(sb_in[...], axis=0)
     for p in chips:
         send(5, sc_all.at[z], sc_all.at[z], {"tensor": 2 * p + core})
-    rs_step(3)
+    rs_step(3, True)
+    rs_step(4, False)
 
     arrived(3, g_all.at[pl.ds(0, T - 1)])
     gram = jnp.sum(g_all[...], axis=0)
@@ -319,57 +340,71 @@
 
     arrived(5, sc_all.at[pl.ds(0, Z - 1)])
     sd_ref[...] = jnp.sum(sc_all[...], axis=0)
-    tile(sfin_ref, me_g, core * 16)[...] = sd_ref[...]
+    tile(sfin_ref, me_g, core * H)[...] = sd_ref[...]
     for p in groups:
-        send(6, sd_ref, tile(sfin_ref, me_g, core * 16), {"group": p})
+        send(6, sd_ref, tile(sfin_ref, me_g, core * H), {"group": p})
+    rs_step(4, True)
 
     pt = jnp.dot(inv_ref[...], rt_ref[...], precision=lax.Precision.HIGHEST, preferred_element_type=F32)
     pt_ref[...] = pt
     hi = pt.astype(BF16)
     lo = (pt - hi.astype(F32)).astype(BF16)
-    p3_ref[...] = -jnp.concatenate([hi, hi, lo], axis=0)
-    rs_step(4)
+    p3_ref[...] = -jnp.concatenate([hi, hi, lo], axis=0).T
     back = dot_nt(cf_ref[0].reshape(F, H), w_ref[:, :H]) + dot_nt(cf_ref[1].reshape(F, H), w_ref[:, H:])
     ig_ref[...] = back.astype(BF16)
 
-    arrived(6, sb_in.at[pl.ds(0, G - 1)])
-    mine = sfin_ref.at[rank_rows(core)]
-    se_copy = remote(mine, mine, sib_send.at[4], sib_recv.at[4], sib)
-    se_copy.start()
-
-    rs_copy(0, 4).wait_recv()
-    rs_copy(1, 4).wait_recv()
+    for k in range(PIECES):
+        for direction in (0, 1):
+            for h in (0, 1):
+                land_copy(direction, h, k).wait_send()
+            for s in range(2, 5):
+                if s < 4 or goes_round(direction, k):
+                    ag_copy(direction, s, k).wait_send()
+    for s in range(1, 4):
+        for direction in (0, 1):
+            for q in (0, 1):
+                if s > 1 or q == direction:
+                    rs_copy(direction, s, q).wait_send()
+    px_copy.wait_send()
+    y_copy.wait_send()
+    sa_copy.wait_send()
+    for d in range(1, Z):
+        for q in (0, 1):
+            sib_copy(d, q).wait_send()
+    left_here(0, cq_all.at[pl.ds(0, T - 1)])
+
+    @pl.when(me_g < TILES)
+    def _():
+        left_here(1, r_in.at[pl.ds(0, TILES - 1)])
+        left_here(2, r_in.at[pl.ds(0, G - 1)])
+
+    @pl.when(me_g >= TILES)
+    def _():
+        left_here(1, r_in.at[pl.ds(0, TILES)])
+
+    left_here(3, g_all.at[pl.ds(0, T - 1)])
+    left_here(4, sb_in.at[pl.ds(0, G - 1)])
+    left_here(5, sc_all.at[pl.ds(0, Z - 1)])
+
+    for direction in (0, 1):
+        for q in (0, 1):
+            rs_copy(direction, 4, q).wait_recv()
     total = part_ref[z] + rsl_in[3].astype(F32) + rsr_in[3].astype(F32)
     fin_out[...] = jnp.where(core == 0, total[OWN:], total[:OWN]).astype(BF16)
     fin_copy = remote(fin_out, fin_in, sib_send.at[5], sib_recv.at[5], sib)
     fin_copy.start()
     proj_ref[:, half(core)] = jnp.where(core == 0, total[:OWN], total[OWN:]).astype(BF16)
+    arrived(6, sb_in.at[pl.ds(0, G - 1)])
+    mine = sfin_ref.at[:, half(core)]
+    se_copy = remote(mine, mine, sib_send.at[4], sib_recv.at[4], sib)
+    se_copy.start()
+
     se_copy.wait()
     fin_copy.wait()
     proj_ref[:, half(other)] = fin_in[...]
-
-    for q in (0, 1):
-        for s in range(1, 5):
-            for direction in (0, 1):
-                if s < 4 or direction == q:
-                    ag_copy(direction, s, q).wait_send()
-    for s in range(1, 5):
-        for direction in (0, 1):
-            rs_copy(direction, s).wait_send()
-    left_here(0, cq_all.at[pl.ds(0, T - 1)])
-
-    @pl.when(me_g < TILES)
-    def _():
-        left_here(1, r_in.at[pl.ds(0, TILES - 1)])
-        left_here(2, r_in.at[pl.ds(0, G - 1)])
-
-    @pl.when(me_g >= TILES)
-    def _():
-        left_here(1, r_in.at[pl.ds(0, TILES)])
-
-    left_here(3, g_all.at[pl.ds(0, T - 1)])
-    left_here(4, sb_in.at[pl.ds(0, G - 1)])
-    left_here(5, sc_all.at[pl.ds(0, Z - 1)])
+    for direction in (0, 1):
+        for q in (0, 1):
+            rs_copy(direction, 4, q).wait_send()
     left_here(6, sb_in.at[pl.ds(0, G - 1)])
 
 
@@ -383,7 +418,7 @@
             jax.ShapeDtypeStruct((F, F), BF16),
             jax.ShapeDtypeStruct((OWN, N), BF16),
             jax.ShapeDtypeStruct((R, F), F32),
-            jax.ShapeDtypeStruct((3 * R, F), BF16),
+            jax.ShapeDtypeStruct((F, 3 * R), BF16),
             jax.ShapeDtypeStruct((R, R), F32),
             jax.ShapeDtypeStruct((R, N), F32),
         ),
@@ -394,13 +429,13 @@
             v((F, F), BF16), v((F, N), BF16), v((F, N), BF16), v((3 * R, N), BF16),
             v((3 * R, F), BF16), v((F, R), F32), v((R, F), F32), v((R, F), F32),
             v((T, 8, 128), F32), v((TILES, 8, 128), F32), v((G, 8, 128), F32), v((TILES, 8, 128), F32), v((T, 8, 128), F32),
-            v((R, N), F32), v((16, N), F32), v((16, N), F32), v((G, 8, 384), F32), v((Z, 8, 384), F32),
+            v((R, F), F32), v((R, F), F32), v((R, N), F32), v((R, H), F32), v((R, H), F32), v((G, 8, 384), F32), v((Z, 8, 384), F32),
             v((8, 384), F32), v((2, Z, CHIP, H), BF16),
-            v((OWN, H), BF16), v((Z, CHIP, H), F32), v((F, H), BF16), v((F, H), BF16),
+            v((2, 2, OWN, H), BF16), v((OWN, N), BF16), v((Z, CHIP, H), F32), v((F, H), BF16), v((F, H), BF16),
             v((4, CHIP, H), BF16), v((4, CHIP, H), BF16), v((4, CHIP, H), BF16), v((4, CHIP, H), BF16),
             v((OWN, H), BF16), v((OWN, H), BF16),
             dma((8,)), dma((7,)), dma((7,)),
-            dma((6,)), dma((6,)), dma((2, 4, 2)), dma((2, 4, 2)), dma((Z, 2)), dma((Z, 2)), dma((2, 4)), dma((2, 4)),
+            dma((6,)), dma((6,)), dma((2, 2, PIECES)), dma((2, 2, PIECES)), dma((2, 3, PIECES)), dma((2, 3, PIECES)), dma((Z, 2)), dma((Z, 2)), dma((2, 4, 2)), dma((2, 4, 2)),
         ],
         compiler_params=pltpu.CompilerParams(
             collective_id=0, has_side_effects=True, vmem_limit_bytes=40 * 1024 * 1024
@@ -424,7 +459,7 @@
     ]
     for cp in copies:
         cp.start()
-    p3 = p3_ref[...].T
+    p3 = p3_ref[...]
     for i in range(N // COLS):
         cols = pl.ds(i * COLS, COLS)
         qt = jnp.dot(inv_ref[...], s_ref[:, cols] * (1.0 / G), precision=lax.Precision.HIGHEST, preferred_element_type=F32)

time: 56 us -> 51.2 us (0.914)
  Pallas kernels: 55.3 us -> 50.5 us
    pallas_call x1, Pallas kernels: 52.1 us -> 47.5 us  [communicate(): pl.pallas_call(comm_kernel, out_shape=(jax.ShapeDtypeStruct((F, N), F32),...]
where the time goes in v3:
time: 51.2 us; the launch traced here: 51.1 us
  Pallas kernels  50.5 us (99%)
  between operations  0.64 us (1%)
    pallas_call x1, Pallas kernels, communicate(): pl.pallas_call(comm_kernel, out_shape=(jax.ShapeDtypeStruct((F, N), F32),...  47.5 us
    pallas_call x1, Pallas kernels, finish(): pl.pallas_call(finish_kernel, out_shape=(jax.ShapeDtypeStruct((F, N), F32...  2.95 us

profile of v3, /device:TPU:1, one launch (start us, length us, event | category | flops | bytes accessed | tf_op | source)
XLA Modules:
  0.0 51.1 jit_solution(5882909365691172549)
XLA Ops:
  0.6 47.5 %communicate.1 = (f32[384,3072]{1,0:T(8,128)S(1)}, bf16[384,384]{1,0:T(8,128)(2,1)S(1)}, bf16[24,3072]{1,0:T(8,128)(2,1)S(1)}, f32[32,384]{1,0:T(8,128)S(1)}, bf...) custom-call(bf16[384,384]{1,0:T(8,128)(2,1)} %a_hbm.1, bf16[24,3072]{1,0:T(8,128)(2,1)} %c_hbm.1, ...), custom_call_target="tpu_custom_call" | custom-call | tf_op jit(solution)/shard_map/communicate/pallas_call | solution.py:414
  48.2 2.9 %finish.1 = (f32[384,3072]{1,0:T(8,128)}, bf16[384,384]{1,0:T(8,128)(2,1)}, bf16[24,3072]{1,0:T(8,128)(2,1)}, f32[32,384]{1,0:T(8,128)}, f32[32,3072]{1,0:T(8,128)}) custom-call(f32[384,3072]{1,0:T(8,128)S(1)} %get-tuple-element.17.m_ref, bf16[384,384]{1,0:T(8,128)(2,1)S(1)} %get-tuple-element.18.ig_ref, bf16[24,3072]{1,0:T(8,128)(2,1)S(1)} %get-tuple-element.19.proj_ref, ...), custom_call_target="tpu_custom_call" | custom-call | tf_op jit(solution)/shard_map/finish/pallas_call | solution.py:482

commit v4 on v3

--- a/solution.py
+++ b/solution.py
@@ -347,8 +347,9 @@
 
     pt = jnp.dot(inv_ref[...], rt_ref[...], precision=lax.Precision.HIGHEST, preferred_element_type=F32)
     pt_ref[...] = pt
-    hi = pt.astype(BF16)
-    lo = (pt - hi.astype(F32)).astype(BF16)
+    vt = jnp.dot(inv_ref[...].T, pt * (1.0 / G), precision=lax.Precision.HIGHEST, preferred_element_type=F32)
+    hi = vt.astype(BF16)
+    lo = (vt - hi.astype(F32)).astype(BF16)
     p3_ref[...] = -jnp.concatenate([hi, hi, lo], axis=0).T
     back = dot_nt(cf_ref[0].reshape(F, H), w_ref[:, :H]) + dot_nt(cf_ref[1].reshape(F, H), w_ref[:, H:])
     ig_ref[...] = back.astype(BF16)
@@ -386,6 +387,11 @@
     left_here(4, sb_in.at[pl.ds(0, G - 1)])
     left_here(5, sc_all.at[pl.ds(0, Z - 1)])
 
+    arrived(6, sb_in.at[pl.ds(0, G - 1)])
+    mine = sfin_ref.at[:, half(core)]
+    se_copy = remote(mine, mine, sib_send.at[4], sib_recv.at[4], sib)
+    se_copy.start()
+
     for direction in (0, 1):
         for q in (0, 1):
             rs_copy(direction, 4, q).wait_recv()
@@ -394,11 +400,6 @@
     fin_copy = remote(fin_out, fin_in, sib_send.at[5], sib_recv.at[5], sib)
     fin_copy.start()
     proj_ref[:, half(core)] = jnp.where(core == 0, total[:OWN], total[OWN:]).astype(BF16)
-    arrived(6, sb_in.at[pl.ds(0, G - 1)])
-    mine = sfin_ref.at[:, half(core)]
-    se_copy = remote(mine, mine, sib_send.at[4], sib_recv.at[4], sib)
-    se_copy.start()
-
     se_copy.wait()
     fin_copy.wait()
     proj_ref[:, half(other)] = fin_in[...]
@@ -444,7 +445,7 @@
     )(attended, cotangent, right_init_t, out_weight, feedback)
 
 
-COLS = 512
+CHUNKS = ((0, 256), (256, 768), (768, 1280), (1280, 1792), (1792, 2304), (2304, 2816), (2816, 3072))
 
 
 def finish_kernel(
@@ -460,16 +461,20 @@
     for cp in copies:
         cp.start()
     p3 = p3_ref[...]
-    for i in range(N // COLS):
-        cols = pl.ds(i * COLS, COLS)
-        qt = jnp.dot(inv_ref[...], s_ref[:, cols] * (1.0 / G), precision=lax.Precision.HIGHEST, preferred_element_type=F32)
-        qt_ref[:, cols] = qt
-        hi = qt.astype(BF16)
-        lo = (qt - hi.astype(F32)).astype(BF16)
-        err_ref[i] = m_ref[:, cols] + dot(p3, jnp.concatenate([hi, lo, hi], axis=0))
-        cp = pltpu.make_async_copy(err_ref.at[i], err_hbm.at[:, cols], err_sem.at[i])
+    for i, (first, last) in enumerate(CHUNKS):
+        cols = pl.ds(first, last - first)
+        s = s_ref[:, cols]
+        hi = s.astype(BF16)
+        lo = (s - hi.astype(F32)).astype(BF16)
+        err_ref[:, cols] = m_ref[:, cols] + dot(p3, jnp.concatenate([hi, lo, hi], axis=0))
+        cp = pltpu.make_async_copy(err_ref.at[:, cols], err_hbm.at[:, cols], err_sem.at[i])
         cp.start()
         copies.append(cp)
+    for first, last in CHUNKS:
+        cols = pl.ds(first, last - first)
+        qt_ref[:, cols] = jnp.dot(
+            inv_ref[...], s_ref[:, cols] * (1.0 / G), precision=lax.Precision.HIGHEST, preferred_element_type=F32
+        )
     cp = pltpu.make_async_copy(qt_ref, qt_hbm, sem.at[3])
     cp.start()
     copies.append(cp)
@@ -491,8 +496,8 @@
         in_specs=[vmem] * 7,
         out_specs=[hbm] * 5,
         scratch_shapes=[
-            pltpu.VMEM((N // COLS, F, COLS), F32), pltpu.VMEM((R, N), F32),
-            pltpu.SemaphoreType.DMA((4,)), pltpu.SemaphoreType.DMA((N // COLS,)),
+            pltpu.VMEM((F, N), F32), pltpu.VMEM((R, N), F32),
+            pltpu.SemaphoreType.DMA((4,)), pltpu.SemaphoreType.DMA((len(CHUNKS),)),
         ],
         compiler_params=pltpu.CompilerParams(vmem_limit_bytes=32 * 1024 * 1024),
         name="finish",

time: 51.2 us -> 51.1 us (level)
  no operation moved by 1% of the time
where the time goes in v4:
time: 51.1 us; the launch traced here: 51 us
  Pallas kernels  50.3 us (98%)
  between operations  0.64 us (1%)
    pallas_call x1, Pallas kernels, communicate(): pl.pallas_call(comm_kernel, out_shape=(jax.ShapeDtypeStruct((F, N), F32),...  47.6 us
    pallas_call x1, Pallas kernels, finish(): pl.pallas_call(finish_kernel, out_shape=(jax.ShapeDtypeStruct((F, N), F32...  2.69 us

profile of v4, /device:TPU:1, one launch (start us, length us, event | category | flops | bytes accessed | tf_op | source)
XLA Modules:
  0.0 51.0 jit_solution(9429929972472070330)
XLA Ops:
  0.6 47.6 %communicate.1 = (f32[384,3072]{1,0:T(8,128)S(1)}, bf16[384,384]{1,0:T(8,128)(2,1)S(1)}, bf16[24,3072]{1,0:T(8,128)(2,1)S(1)}, f32[32,384]{1,0:T(8,128)S(1)}, bf...) custom-call(bf16[384,384]{1,0:T(8,128)(2,1)} %a_hbm.1, bf16[24,3072]{1,0:T(8,128)(2,1)} %c_hbm.1, ...), custom_call_target="tpu_custom_call" | custom-call | tf_op jit(solution)/shard_map/communicate/pallas_call | solution.py:415
  48.3 2.7 %finish.1 = (f32[384,3072]{1,0:T(8,128)}, bf16[384,384]{1,0:T(8,128)(2,1)}, bf16[24,3072]{1,0:T(8,128)(2,1)}, f32[32,384]{1,0:T(8,128)}, f32[32,3072]{1,0:T(8,128)}) custom-call(f32[384,3072]{1,0:T(8,128)S(1)} %get-tuple-element.17.m_ref, bf16[384,384]{1,0:T(8,128)(2,1)S(1)} %get-tuple-element.18.ig_ref, bf16[24,3072]{1,0:T(8,128)(2,1)S(1)} %get-tuple-element.19.proj_ref, ...), custom_call_target="tpu_custom_call" | custom-call | tf_op jit(solution)/shard_map/finish/pallas_call | solution.py:487
